TPU v7x, 32 devices: a whole 2x2x4 slice. The times are simulated.
32 devices in a mesh: dp: 8 (over z, y), mp: 4 (over x, core).
Axes of the slice: x: 2, y: 2, z: 4, core: 2. Of those that a mesh axis runs over, the one named last changes fastest.
Arguments:
- tokens: bfloat16 [2, 8192, 1024], P(None, ('dp', 'mp')), may hold values from -6 to 6
- lengths: int32 [8, 2, 2], P('dp'), may hold values from 0 to 1024, as said below
- cotangent: bfloat16 [2, 8192, 1024], P(None, ('dp', 'mp')), may hold values from -6 to 6
- attn_gain: float32 [1024], replicated, may hold values from 0.5 to 1.5
- in_weights: bfloat16 [1024, 4, 1024], P(None, None, 'mp'), may hold values from -0.1875 to 0.1875
- ssm_rate: float32 [16, 1024], P(None, 'mp'), may hold values from 0.00048828125 to 0.015625
- ssm_input: float32 [16, 1024], P(None, 'mp'), may hold values from -4 to 4
- ssm_output: float32 [16, 1024], P(None, 'mp'), may hold values from -1.5 to 1.5
- ctx_weights: bfloat16 [8, 128, 256], P('mp'), may hold values from -0.5 to 0.5
- out_weights: bfloat16 [1024, 1024], P('mp'), may hold values from -1.5 to 1.5
- mlp_gain: float32 [1024], replicated, may hold values from 0.5 to 1.5
- up_weights: bfloat16 [1024, 4096], P(None, 'mp'), may hold values from -0.1875 to 0.1875
- down_weights: bfloat16 [4096, 1024], P('mp'), may hold values from -0.09375 to 0.09375
Outputs:
- mixed: bfloat16 [2, 8192, 1024], P(None, ('dp', 'mp'))
- grad_tokens: float32 [2, 8192, 1024], P(None, ('dp', 'mp'))
- grad_attn_gain: float32 [1024], replicated
- grad_in_weights: float32 [1024, 4, 1024], P(None, None, 'mp')
- grad_ssm_rate: float32 [16, 1024], P(None, 'mp')
- grad_ssm_input: float32 [16, 1024], P(None, 'mp')
- grad_ssm_output: float32 [16, 1024], P(None, 'mp')
- grad_ctx_weights: float32 [8, 128, 256], P('mp')
- grad_out_weights: float32 [1024, 1024], P('mp')
- grad_mlp_gain: float32 [1024], replicated
- grad_up_weights: float32 [1024, 4096], P(None, 'mp')
- grad_down_weights: float32 [4096, 1024], P('mp')
Inputs may be any that keep to these rules, and one draw needn't show every extreme that they name: `lengths`: entry 0 is a document of 512 tokens or more; entry 1 is 0 or a second document of 512 tokens or more; each document starts on a block of 512 rows and both fit in 1024 rows; in micro-batch 0 the first document of every group is longer than 768 tokens.
All inputs are finite; a program needn't handle non-finite values.
Results may differ from a plain program's by a relative error of at most 0.012.
Values may be sent and summed in bfloat16 or wider, within the bound.
A program may use at most 192 MiB of HBM per device.

v0:
```python
import math

import jax
import jax.numpy as jnp
from jax import lax
from jax.sharding import PartitionSpec as P

HD = 128
BLK = 512
CTX = 128


highest = lax.Precision.HIGHEST


def rms_norm(values, gain):
    return values * lax.rsqrt(jnp.mean(values * values, axis=-1, keepdims=True) + 1e-05) * gain


def gelu_value(values):
    return jax.nn.gelu(values, approximate=True)


def block_layout(doc_lengths, nblocks):
    first_blocks = (doc_lengths[0] + BLK - 1) // BLK
    second_blocks = (doc_lengths[1] + BLK - 1) // BLK
    block_index = jnp.arange(nblocks, dtype=jnp.int32)
    document = jnp.where(
        block_index < first_blocks, 0, jnp.where(block_index < first_blocks + second_blocks, 1, 2)
    )
    start_block = jnp.where(document == 0, 0, first_blocks)
    doc_extent = jnp.where(
        document == 0, doc_lengths[0], jnp.where(document == 1, doc_lengths[1], 0)
    )
    within_doc = (block_index - start_block)[:, None] * BLK + jnp.arange(BLK, dtype=jnp.int32)[
        None, :
    ]
    token_valid = within_doc < doc_extent[:, None]
    linked = jnp.concatenate([jnp.zeros((1,), dtype=bool), document[1:] == document[:-1]])
    return (token_valid, linked.astype(jnp.float32))


def ssm_context(driver, rate, input_coef, output_coef, linked):
    chans = driver.shape[1]
    nblocks = driver.shape[0] // BLK
    head_len = BLK - CTX
    blocks = driver.reshape(nblocks, BLK, chans)
    in_gain = input_coef * jnp.sqrt(1.0 - jnp.exp(-2.0 * rate))
    head_pos = jnp.arange(head_len, dtype=jnp.float32)
    head_table = jnp.exp(-rate[:, :, None] * (head_len - 1.0 - head_pos)) * in_gain[:, :, None]
    head_decay = jnp.exp(-rate * head_len)
    tail_pos = jnp.arange(CTX, dtype=jnp.float32)
    rising = jnp.exp(rate[None] * tail_pos[:, None, None]) * in_gain[None]
    falling = jnp.exp(-rate[None] * tail_pos[:, None, None])
    lower = (tail_pos[:, None] >= tail_pos[None, :]).astype(jnp.float32)
    single = jnp.exp(-rate)

    def advance(state, packed):
        block, keep = packed
        state = state * keep
        middle = head_decay * state + jnp.einsum(
            "ncj,jc->nc", head_table, block[:head_len], precision=highest
        )
        weighted = rising * block[head_len:, None, :]
        prefix = jnp.dot(lower, weighted.reshape(CTX, -1), precision=highest).reshape(
            weighted.shape
        )
        states = falling * (single[None] * middle[None] + prefix)
        context = jnp.sum(output_coef[None] * states, axis=1)
        return (states[-1], context)

    _, contexts = lax.scan(
        jax.checkpoint(advance), jnp.zeros(rate.shape, jnp.float32), (blocks, linked)
    )
    return jnp.concatenate([jnp.zeros_like(contexts[:1]), contexts[:-1]], axis=0)


def block_scores(query_b, key_b, ckey_b, keep, valid_b):
    scale = 1.0 / math.sqrt(HD)
    scores = (
        jnp.concatenate(
            [
                jnp.einsum("thd,jhd->htj", query_b, ckey_b, preferred_element_type=jnp.float32),
                jnp.einsum("thd,jhd->htj", query_b, key_b, preferred_element_type=jnp.float32),
            ],
            axis=-1,
        )
        * scale
    )
    places = jnp.arange(BLK, dtype=jnp.int32)
    earlier = places[None, :] <= places[:, None]
    seen = earlier & (valid_b[None, :] | (places[None, :] == places[:, None]))
    linked_keys = jnp.broadcast_to(keep > 0.5, (BLK, CTX))
    allowed = jnp.concatenate([linked_keys, seen], axis=1)
    return jnp.where(allowed[None], scores, -1e30)


def attend_forward(packed):
    query_b, key_b, value_b, ckey_b, cval_b, keep, valid_b = packed
    scores = block_scores(query_b, key_b, ckey_b, keep, valid_b)
    peak_score = jnp.max(scores, axis=-1, keepdims=True)
    weights = jnp.exp(scores - peak_score)
    denominator = jnp.sum(weights, axis=-1, keepdims=True)
    probs = (weights / denominator).astype(jnp.bfloat16)
    result = jnp.einsum(
        "htj,jhd->thd", probs[:, :, :CTX], cval_b, preferred_element_type=jnp.float32
    ) + jnp.einsum("htj,jhd->thd", probs[:, :, CTX:], value_b, preferred_element_type=jnp.float32)
    return (result.astype(jnp.bfloat16), (peak_score + jnp.log(denominator))[..., 0])


def attend_backward(packed):
    query_b, key_b, value_b, ckey_b, cval_b, keep, valid_b, log_sum, grad_b = packed
    scale = 1.0 / math.sqrt(HD)
    scores = block_scores(query_b, key_b, ckey_b, keep, valid_b)
    probs = jnp.exp(scores - log_sum[..., None])
    low_probs = probs.astype(jnp.bfloat16)
    grad_probs = jnp.concatenate(
        [
            jnp.einsum("thd,jhd->htj", grad_b, cval_b, preferred_element_type=jnp.float32),
            jnp.einsum("thd,jhd->htj", grad_b, value_b, preferred_element_type=jnp.float32),
        ],
        axis=-1,
    )
    grad_cval = jnp.einsum(
        "htj,thd->jhd", low_probs[:, :, :CTX], grad_b, preferred_element_type=jnp.float32
    )
    grad_value = jnp.einsum(
        "htj,thd->jhd", low_probs[:, :, CTX:], grad_b, preferred_element_type=jnp.float32
    )
    grad_scores = probs * (grad_probs - jnp.sum(grad_probs * probs, axis=-1, keepdims=True))
    grad_scores = grad_scores.astype(jnp.bfloat16)
    grad_query = (
        jnp.einsum(
            "htj,jhd->thd", grad_scores[:, :, :CTX], ckey_b, preferred_element_type=jnp.float32
        )
        + jnp.einsum(
            "htj,jhd->thd", grad_scores[:, :, CTX:], key_b, preferred_element_type=jnp.float32
        )
    ) * scale
    grad_ckey = (
        jnp.einsum(
            "htj,thd->jhd", grad_scores[:, :, :CTX], query_b, preferred_element_type=jnp.float32
        )
        * scale
    )
    grad_key = (
        jnp.einsum(
            "htj,thd->jhd", grad_scores[:, :, CTX:], query_b, preferred_element_type=jnp.float32
        )
        * scale
    )
    return (grad_query, grad_key, grad_value, grad_ckey, grad_cval)


def mixer_forward(
    normed_full, in_weights, ssm_rate, ssm_input, ssm_output, ctx_weights, token_valid, linked
):
    row_count = normed_full.shape[0]
    chans = in_weights.shape[2]
    heads = chans // HD
    nblocks = row_count // BLK
    flat_weights = in_weights.reshape(in_weights.shape[0], 4 * chans)
    projected = jnp.dot(normed_full, flat_weights, preferred_element_type=jnp.float32).reshape(
        row_count, 4, chans
    )
    queries = projected[:, 0].astype(jnp.bfloat16)
    keys_tok = projected[:, 1].astype(jnp.bfloat16)
    values_tok = projected[:, 2].astype(jnp.bfloat16)
    driver = projected[:, 3]
    context = ssm_context(driver, ssm_rate, ssm_input, ssm_output, linked).astype(jnp.bfloat16)
    ctx_heads = context.reshape(nblocks, CTX, heads, HD)
    ctx_keys = jnp.einsum(
        "bjhd,hde->bjhe", ctx_heads, ctx_weights[:, :, :HD], preferred_element_type=jnp.float32
    ).astype(jnp.bfloat16)
    ctx_vals = jnp.einsum(
        "bjhd,hde->bjhe", ctx_heads, ctx_weights[:, :, HD:], preferred_element_type=jnp.float32
    ).astype(jnp.bfloat16)
    block_shape = (nblocks, BLK, heads, HD)
    heads_out, log_sums = lax.map(
        attend_forward,
        (
            queries.reshape(block_shape),
            keys_tok.reshape(block_shape),
            values_tok.reshape(block_shape),
            ctx_keys,
            ctx_vals,
            linked,
            token_valid,
        ),
    )
    return (
        queries,
        keys_tok,
        values_tok,
        driver,
        context,
        ctx_keys,
        ctx_vals,
        log_sums,
        heads_out.reshape(row_count, chans),
    )


def mixer_backward(
    normed_full,
    saved,
    grad_heads,
    in_weights,
    ssm_rate,
    ssm_input,
    ssm_output,
    ctx_weights,
    token_valid,
    linked,
):
    queries, keys_tok, values_tok, driver, context, ctx_keys, ctx_vals, log_sums, heads_out = saved
    row_count, chans = queries.shape
    heads = chans // HD
    nblocks = row_count // BLK
    block_shape = (nblocks, BLK, heads, HD)
    grad_query, grad_key, grad_value, grad_ckey, grad_cval = lax.map(
        attend_backward,
        (
            queries.reshape(block_shape),
            keys_tok.reshape(block_shape),
            values_tok.reshape(block_shape),
            ctx_keys,
            ctx_vals,
            linked,
            token_valid,
            log_sums,
            grad_heads.reshape(block_shape),
        ),
    )
    grad_ckey = grad_ckey.astype(jnp.bfloat16)
    grad_cval = grad_cval.astype(jnp.bfloat16)
    ctx_heads = context.reshape(nblocks, CTX, heads, HD)
    grad_ctx_weights = jnp.concatenate(
        [
            jnp.einsum("bjhd,bjhe->hde", ctx_heads, grad_ckey, preferred_element_type=jnp.float32),
            jnp.einsum("bjhd,bjhe->hde", ctx_heads, grad_cval, preferred_element_type=jnp.float32),
        ],
        axis=-1,
    )
    grad_context = jnp.einsum(
        "bjhe,hde->bjhd", grad_ckey, ctx_weights[:, :, :HD], preferred_element_type=jnp.float32
    ) + jnp.einsum(
        "bjhe,hde->bjhd", grad_cval, ctx_weights[:, :, HD:], preferred_element_type=jnp.float32
    )
    grad_context = grad_context.reshape(nblocks, CTX, chans)

    def state_space(drive, rate, input_coef, output_coef):
        return ssm_context(drive, rate, input_coef, output_coef, linked)

    _, state_pull = jax.vjp(state_space, driver, ssm_rate, ssm_input, ssm_output)
    grad_driver, grad_rate, grad_input, grad_output = state_pull(grad_context)
    grad_projected = jnp.stack(
        [
            grad_query.reshape(row_count, chans).astype(jnp.bfloat16),
            grad_key.reshape(row_count, chans).astype(jnp.bfloat16),
            grad_value.reshape(row_count, chans).astype(jnp.bfloat16),
            grad_driver.astype(jnp.bfloat16),
        ],
        axis=1,
    ).reshape(row_count, 4 * chans)
    flat_weights = in_weights.reshape(in_weights.shape[0], 4 * chans)
    grad_in_weights = jnp.einsum(
        "rd,re->de", normed_full, grad_projected, preferred_element_type=jnp.float32
    ).reshape(in_weights.shape)
    grad_normed_part = jnp.einsum(
        "re,de->rd", grad_projected, flat_weights, preferred_element_type=jnp.float32
    )
    return (
        grad_normed_part,
        (grad_in_weights, grad_rate, grad_input, grad_output, grad_ctx_weights),
    )


def ffn_forward(normed_two_full, up_weights):
    before = jnp.dot(normed_two_full, up_weights, preferred_element_type=jnp.float32)
    return (before, gelu_value(before).astype(jnp.bfloat16))


def body(
    tokens,
    lengths,
    cotangent,
    attn_gain,
    in_weights,
    ssm_rate,
    ssm_input,
    ssm_output,
    ctx_weights,
    out_weights,
    mlp_gain,
    up_weights,
    down_weights,
):
    micro_count = tokens.shape[0]
    group_rows = tokens.shape[1] * lax.axis_size("mp")
    nblocks = group_rows // BLK
    shapes = (
        in_weights.shape,
        ssm_rate.shape,
        ssm_input.shape,
        ssm_output.shape,
        ctx_weights.shape,
        out_weights.shape,
        up_weights.shape,
        down_weights.shape,
    )
    totals = tuple((jnp.zeros(shape, jnp.float32) for shape in shapes))
    gain_first = jnp.zeros(attn_gain.shape, jnp.float32)
    gain_second = jnp.zeros(mlp_gain.shape, jnp.float32)
    mixed_list = []
    grad_list = []
    for micro in range(micro_count):
        local_in = tokens[micro].astype(jnp.float32)
        token_valid, linked = block_layout(lengths[0, micro], nblocks)
        normed, norm_pull = jax.vjp(rms_norm, local_in, attn_gain)
        normed_low = normed.astype(jnp.bfloat16)
        normed_full = lax.all_gather(normed_low, "mp", axis=0, tiled=True)
        saved = mixer_forward(
            normed_full,
            in_weights,
            ssm_rate,
            ssm_input,
            ssm_output,
            ctx_weights,
            token_valid,
            linked,
        )
        attn_part = jnp.dot(saved[-1], out_weights, preferred_element_type=jnp.float32)
        middle = local_in + lax.psum_scatter(attn_part, "mp", scatter_dimension=0, tiled=True)
        normed_two, norm_two_pull = jax.vjp(rms_norm, middle, mlp_gain)
        normed_two_low = normed_two.astype(jnp.bfloat16)
        normed_two_full = lax.all_gather(normed_two_low, "mp", axis=0, tiled=True)
        before, hidden = ffn_forward(normed_two_full, up_weights)
        ffn_part = jnp.dot(hidden, down_weights, preferred_element_type=jnp.float32)
        result = middle + lax.psum_scatter(
            ffn_part.astype(jnp.bfloat16), "mp", scatter_dimension=0, tiled=True
        ).astype(jnp.float32)
        mixed_list.append(result.astype(jnp.bfloat16))
        grad_out = cotangent[micro]
        grad_full = lax.all_gather(grad_out, "mp", axis=0, tiled=True)
        grad_down = jnp.einsum("rf,rd->fd", hidden, grad_full, preferred_element_type=jnp.float32)
        grad_hidden = jnp.einsum(
            "rd,fd->rf", grad_full, down_weights, preferred_element_type=jnp.float32
        )
        _, gelu_pull = jax.vjp(gelu_value, before)
        grad_before = gelu_pull(grad_hidden)[0].astype(jnp.bfloat16)
        grad_up = jnp.einsum(
            "rd,rf->df", normed_two_full, grad_before, preferred_element_type=jnp.float32
        )
        grad_normed_two_part = jnp.einsum(
            "rf,df->rd", grad_before, up_weights, preferred_element_type=jnp.float32
        )
        grad_normed_two = lax.psum_scatter(
            grad_normed_two_part, "mp", scatter_dimension=0, tiled=True
        )
        grad_middle_norm, grad_gain_two = norm_two_pull(grad_normed_two)
        grad_middle = grad_out.astype(jnp.float32) + grad_middle_norm
        grad_branch = lax.all_gather(grad_middle.astype(jnp.bfloat16), "mp", axis=0, tiled=True)
        grad_out_weights = jnp.einsum(
            "rc,rd->cd", saved[-1], grad_branch, preferred_element_type=jnp.float32
        )
        grad_heads = jnp.einsum(
            "rd,cd->rc", grad_branch, out_weights, preferred_element_type=jnp.float32
        ).astype(jnp.bfloat16)
        grad_normed_part, mixer_grads = mixer_backward(
            normed_full,
            saved,
            grad_heads,
            in_weights,
            ssm_rate,
            ssm_input,
            ssm_output,
            ctx_weights,
            token_valid,
            linked,
        )
        grad_normed = lax.psum_scatter(grad_normed_part, "mp", scatter_dimension=0, tiled=True)
        grad_input_norm, grad_gain_one = norm_pull(grad_normed)
        grad_list.append(grad_middle + grad_input_norm)
        grads = (
            mixer_grads[0],
            mixer_grads[1],
            mixer_grads[2],
            mixer_grads[3],
            mixer_grads[4],
            grad_out_weights,
            grad_up,
            grad_down,
        )
        grads = lax.psum(
            (grads[0], grads[1], grads[2], grads[3], grads[4], grads[5], grads[6], grads[7]), "dp"
        )
        totals = tuple((left + right for left, right in zip(totals, grads)))
        gain_first = gain_first + grad_gain_one
        gain_second = gain_second + grad_gain_two
    gain_attn, gain_mlp = lax.psum((gain_first, gain_second), ("dp", "mp"))
    return (
        jnp.stack(mixed_list),
        jnp.stack(grad_list),
        gain_attn,
        totals[0],
        totals[1],
        totals[2],
        totals[3],
        totals[4],
        totals[5],
        gain_mlp,
        totals[6],
        totals[7],
    )


def solution(mesh):
    placed = (
        P(None, ("dp", "mp"), None),
        P("dp", None, None),
        P(None, ("dp", "mp"), None),
        P(),
        P(None, None, "mp"),
        P(None, "mp"),
        P(None, "mp"),
        P(None, "mp"),
        P("mp", None, None),
        P("mp", None),
        P(),
        P(None, "mp"),
        P("mp", None),
    )
    return jax.shard_map(
        body,
        mesh=mesh,
        in_specs=placed,
        out_specs=(
            P(None, ("dp", "mp"), None),
            P(None, ("dp", "mp"), None),
            P(),
            P(None, None, "mp"),
            P(None, "mp"),
            P(None, "mp"),
            P(None, "mp"),
            P("mp", None, None),
            P("mp", None),
            P(),
            P(None, "mp"),
            P("mp", None),
        ),
        check_vma=False,
    )
```

profile of v0, /device:TPU:0, one launch (start us, length us, event | category | flops | bytes accessed | tf_op | source)
XLA Modules:
  0.0 1435.2 jit_solution(17981095325247410870)
XLA Ops:
  45.2 41.8 %while.183 = (s32[]{:T(128)}, f32[16,256]{1,0:T(8,128)}, bf16[2,128,256]{1,2,0:T(8,128)(2,1)}, f32[2]{0:T(128)}, f32[16,256]{1,0:T(8,128)}, /*index=5*/f32[2,512...) while((s32[]{:T(128)}, f32[16,256]{1,0:T(8,128)}, ...), condition=%wide.region_14.15_spmd.clone.clone, body=%wide.region_12.14_spmd.clone.clone.sunk | while | flops 815804416 | bytes 23644036 | solution.py:72
  102.6 29.0 %while.179 = (s32[]{:T(128)}, bf16[2,512,2,128]{3,2,1,0:T(2,128)(2,1)}, f32[2,2,512]{2,1,0:T(2,128)}, bf16[2,128,2,128]{3,1,0,2:T(8,128)(2,1)}, pred[2,512]{1,0:...) while((s32[]{:T(128)}, ...), condition=%wide.region_18.19_spmd, body=%wide.region_15.18_spmd.sunk | while | flops 346684416 | bytes 20614852 | solution.py:179
  151.4 46.0 %while.182 = (s32[]{:T(128)}, f32[16,256]{1,0:T(8,128)}, bf16[2,128,256]{1,2,0:T(8,128)(2,1)}, f32[2]{0:T(128)}, f32[16,256]{1,0:T(8,128)}, /*index=5*/f32[2,512...) while((s32[]{:T(128)}, f32[16,256]{1,0:T(8,128)}, ...), condition=%wide.region_3.4_spmd.clone.clone, body=%wide.region_1.3_spmd.clone.clone.sunk | while | flops 815804416 | bytes 23644036 | solution.py:72
  203.5 29.4 %while.178 = (s32[]{:T(128)}, bf16[2,512,2,128]{3,2,1,0:T(2,128)(2,1)}, f32[2,2,512]{2,1,0:T(2,128)}, bf16[2,128,2,128]{3,1,0,2:T(8,128)(2,1)}, pred[2,512]{1,0:...) while((s32[]{:T(128)}, ...), condition=%wide.region_7.8_spmd, body=%wide.region_4.7_spmd.sunk | while | flops 346684416 | bytes 20614852 | solution.py:179
  237.3 44.7 %reduce-scatter.9.cloned.1.call-done = f32[256,1024]{1,0:T(8,128)} async-done(((f32[1024,1024]{1,0:T(8,128)}), f32[256,1024]{1,0:T(8,128)}) %reduce-scatter.9.cloned.1.call-update) | async-done | bytes 1048592 | tf_op jit(solution)/shard_map/reduce_scatter | solution.py:334
  288.1 21.4 %all-gather.13.cloned.1.call-done = bf16[1024,1024]{1,0:T(8,128)(2,1)} async-done(((bf16[256,1024]{1,0:T(8,128)(2,1)}), bf16[1024,1024]{1,0:T(8,128)(2,1)}) %all-gather.13.cloned.1.call-update) | async-done | bytes 2097168 | tf_op jit(solution)/shard_map/all_gather | solution.py:337
  315.4 18.7 %all-gather.23.cloned.1.call-done = bf16[1,1024,1024]{2,1,0:T(8,128)(2,1)} async-done(((bf16[1,256,1024]{2,1,0:T(8,128)(2,1)}), bf16[1,1024,1024]{2,1,0:T(8,128)(2,1)}) %all-gather.23.cloned.1.call-update) | async-done | bytes 2097168 | tf_op jit(solution)/shard_map/all_gather | solution.py:345
  334.1 7.9 fusion.258
  347.8 44.6 %reduce-scatter.17.cloned.1.call-done = f32[256,1024]{1,0:T(8,128)} async-done(((f32[1024,1024]{1,0:T(8,128)}), f32[256,1024]{1,0:T(8,128)}) %reduce-scatter.17.cloned.1.call-update) | async-done | bytes 1048592 | tf_op jit(solution)/shard_map/reduce_scatter | solution.py:358
  396.7 21.8 %all-gather.17.cloned.1.call-done = bf16[1024,1024]{1,0:T(8,128)(2,1)} async-done(((bf16[256,1024]{1,0:T(8,128)(2,1)}), bf16[1024,1024]{1,0:T(8,128)(2,1)}) %all-gather.17.cloned.1.call-update) | async-done | bytes 2097168 | tf_op jit(solution)/shard_map/all_gather | solution.py:337
  424.4 18.9 %all-gather.25.cloned.1.call-done = bf16[1,1024,1024]{2,1,0:T(8,128)(2,1)} async-done(((bf16[1,256,1024]{2,1,0:T(8,128)(2,1)}), bf16[1,1024,1024]{2,1,0:T(8,128)(2,1)}) %all-gather.25.cloned.1.call-update) | async-done | bytes 2097168 | tf_op jit(solution)/shard_map/all_gather | solution.py:345
  443.3 8.0 fusion.265
  466.2 32.7 %while.185 = (s32[]{:T(128)}, f32[16,256]{1,0:T(8,128)S(1)}, f32[2,16,256]{2,1,0:T(8,128)}, f32[1,16,256]{2,1,0:T(8,128)S(1)}, f32[2]{0:T(128)}, /*index=5*/f32[...) while((s32[]{:T(128)}, f32[16,256]{1,0:T(8,128)S(1)}, ...), condition=%wide.region_42.43_spmd.clone.clone, body=%wide.region_41.42_spmd.clone.clone.sunk | while | flops 813236224 | bytes 13174457 | solution.py:72
  504.1 32.2 %reduce-scatter.15.cloned.1.call-done = bf16[256,1024]{1,0:T(8,128)(2,1)} async-done(((bf16[1024,1024]{1,0:T(8,128)(2,1)}), bf16[256,1024]{1,0:T(8,128)(2,1)}) %reduce-scatter.15.cloned.1.call-update) | async-done | bytes 524304 | tf_op jit(solution)/shard_map/reduce_scatter | solution.py:340
  540.5 31.7 %while.184 = (s32[]{:T(128)}, f32[16,256]{1,0:T(8,128)S(1)}, f32[2,16,256]{2,1,0:T(8,128)S(1)}, f32[1,16,256]{2,1,0:T(8,128)S(1)}, f32[2]{0:T(128)}, /*index=5*/...) while((s32[]{:T(128)}, f32[16,256]{1,0:T(8,128)S(1)}, ...), condition=%wide.region_28.29_spmd.clone.clone, body=%wide.region_27.28_spmd.clone.clone.sunk | while | flops 813236224 | bytes 13174457 | solution.py:72
  579.7 26.7 %while.181 = (s32[]{:T(128)}, bf16[2,512,2,128]{1,3,2,0:T(8,128)(2,1)}, bf16[2,512,2,128]{1,3,2,0:T(8,128)(2,1)}, bf16[2,512,2,128]{1,3,2,0:T(8,128)(2,1)}, bf16...) while((s32[]{:T(128)}, ...), condition=%wide.region_40.41_spmd, body=%wide.region_38.40_spmd.sunk | while | flops 852788864 | bytes 42884076 | solution.py:221
  620.4 26.7 %while.180 = (s32[]{:T(128)}, bf16[2,512,2,128]{1,3,2,0:T(8,128)(2,1)}, bf16[2,512,2,128]{1,3,2,0:T(8,128)(2,1)}, bf16[2,512,2,128]{1,3,2,0:T(8,128)(2,1)}, bf16...) while((s32[]{:T(128)}, ...), condition=%wide.region_26.27_spmd, body=%wide.region_24.26_spmd.sunk | while | flops 852788864 | bytes 42884076 | solution.py:221
  651.8 108.2 %while.186 = (s32[]{:T(128)}, f32[16,256]{1,0:T(8,128)}, f32[16,256,384]{2,1,0:T(8,128)}, f32[128,16,256]{2,0,1:T(8,128)}, f32[16,256]{1,0:T(8,128)}, /*index=5*...) while((s32[]{:T(128)}, f32[16,256]{1,0:T(8,128)}, ...), condition=%wide.region_33.34_spmd.clone.clone.clone, body=%wide.region_29.33_spmd.clone.clone.clone.sunk | while | flops 1635344384 | bytes 81840400 | solution.py:72
  728.2 8.2 multiply_reduce_fusion.53
  771.8 110.5 %while.187 = (s32[]{:T(128)}, f32[16,256]{1,0:T(8,128)}, f32[16,256,384]{2,1,0:T(8,128)}, f32[128,16,256]{2,0,1:T(8,128)}, f32[16,256]{1,0:T(8,128)}, /*index=5*...) while((s32[]{:T(128)}, f32[16,256]{1,0:T(8,128)}, ...), condition=%wide.region_47.48_spmd.clone.clone.clone, body=%wide.region_43.47_spmd.clone.clone.clone.sunk | while | flops 1635344384 | bytes 81774832 | solution.py:72
  850.4 8.2 multiply_reduce_fusion.57
  951.6 38.6 %all-reduce.15 = (f32[16,256]{1,0:T(8,128)}, f32[16,256]{1,0:T(8,128)}, f32[16,256]{1,0:T(8,128)}) all-reduce(f32[16,256]{1,0:T(8,128)S(1)} %get-tuple-element.2570, f32[16,256]{1,0:T(8,128)S(1)} %get-tuple-element.2569, f32[16,256]{1,0:T(8,128)S(1)} %add.484), channel_id=1, replica_groups=mesh['dp'=8,'mp'=4] {'dp'}, use_global_device_ids=true, to_apply=%region_60.61 | all-reduce | flops 12288 | bytes 98304 | tf_op jit(solution)/shard_map/psum | solution.py:395
  992.5 41.9 %all-reduce.14 = (f32[1024]{0:T(1024)}, f32[1024]{0:T(1024)}) all-reduce(f32[1024]{0:T(1024)S(1)} %add.480, f32[1024]{0:T(1024)S(1)} %add.487), channel_id=1, replica_groups=mesh['dp'=8,'mp'=4] {'dp','mp'}, use_global_device_ids=true, to_apply=%region_52.53 | all-reduce | flops 2048 | bytes 16384 | tf_op jit(solution)/shard_map/psum | solution.py:401
  1041.1 370.3 %all-reduce.19.cloned.1.call-done = (f32[1024,4,256]{2,0,1:T(8,128)}, f32[2,128,256]{1,2,0:T(8,128)}, f32[256,1024]{1,0:T(8,128)}, f32[1024,1024]{1,0:T(8,128)}, f32[1024,1024]{1,0:T(8,128)}) async-done(((f32[1024,4,256]{2,0,1:T(8,128)}, f32[2,128,256]{1,2,0:T(8,128)}, f32[256,1024]{1,0:T(8,128)}, f32[1024,1024]{1,0:T(8,128)}, f32[1024,1024]{1,0:T(8,128)}), (f32[1024,4,256]{2,0,1:T(8,128)}, ...) | async-done | bytes 13893648 | tf_op jit(solution)/shard_map/psum | solution.py:395
  (1066 shorter events, 719.8 us)
Async XLA Ops:
  7.2 302.3 %copy-start = (bf16[1024,1024]{1,0:T(8,128)(2,1)S(1)}, bf16[1024,1024]{1,0:T(8,128)(2,1)}, u32[]{:S(2)}) copy-start(bf16[1024,1024]{1,0:T(8,128)(2,1)} %param.44) | copy-start | bytes 6291460
  7.2 30.8 %all-gather.15.cloned.1.call-start = ((), (), s32[]{:S(2)}) async-start(), calls=%async_computation.12 | async-start | bytes 2621440 | tf_op jit(solution)/shard_map/all_gather | solution.py:322
  12.5 123.5 %all-gather.11.cloned.1.call-start = ((), (), s32[]{:S(2)}) async-start(), calls=%async_computation.8 | async-start | bytes 2621440 | tf_op jit(solution)/shard_map/all_gather | solution.py:322
  13.3 224.0 %reduce-scatter.13.cloned.1.call-start = ((), (), s32[]{:S(2)}) async-start(), calls=%async_computation.13 | async-start | bytes 5242880 | tf_op jit(solution)/shard_map/reduce_scatter | solution.py:334
  136.0 146.0 %reduce-scatter.9.cloned.1.call-start = ((), (), s32[]{:S(2)}) async-start(), calls=%async_computation.9 | async-start | bytes 5242880 | tf_op jit(solution)/shard_map/reduce_scatter | solution.py:334
  237.2 72.2 %all-gather.13.cloned.1.call-start = ((), (), s32[]{:S(2)}) async-start(), calls=%async_computation.10 | async-start | bytes 2621440 | tf_op jit(solution)/shard_map/all_gather | solution.py:337
  284.8 251.5 %copy-start.158 = (f32[256]{0:T(256)}, f32[256]{0:T(256)S(1)}, u32[]{:S(2)}) copy-start(f32[256]{0:T(256)S(1)} %fusion.382) | copy-start | bytes 3076
  286.7 47.4 %all-gather.23.cloned.1.call-start = ((), (), s32[]{:S(2)}) async-start(), calls=%async_computation.22 | async-start | bytes 2621440 | tf_op jit(solution)/shard_map/all_gather | solution.py:345
  287.8 104.6 %reduce-scatter.17.cloned.1.call-start = ((), (), s32[]{:S(2)}) async-start(), calls=%async_computation.16 | async-start | bytes 5242880 | tf_op jit(solution)/shard_map/reduce_scatter | solution.py:358
  347.7 70.7 %all-gather.17.cloned.1.call-start = ((), (), s32[]{:S(2)}) async-start(), calls=%async_computation.14 | async-start | bytes 2621440 | tf_op jit(solution)/shard_map/all_gather | solution.py:337
  347.8 188.4 %copy-start.156 = (f32[256]{0:T(256)}, f32[256]{0:T(256)S(1)}, u32[]{:S(2)}) copy-start(f32[256]{0:T(256)S(1)} %fusion.384) | copy-start | bytes 3076
  395.7 47.6 %all-gather.25.cloned.1.call-start = ((), (), s32[]{:S(2)}) async-start(), calls=%async_computation.23 | async-start | bytes 2621440 | tf_op jit(solution)/shard_map/all_gather | solution.py:345
  396.4 105.3 %reduce-scatter.21.cloned.1.call-start = ((), (), s32[]{:S(2)}) async-start(), calls=%async_computation.19 | async-start | bytes 5242880 | tf_op jit(solution)/shard_map/reduce_scatter | solution.py:358
  457.0 79.2 %reduce-scatter.15.cloned.1.call-start = ((), (), s32[]{:S(2)}) async-start(), calls=%async_computation.15 | async-start | bytes 2621440 | tf_op jit(solution)/shard_map/reduce_scatter | solution.py:340
  464.8 107.6 %all-gather.21.cloned.1.call-start = ((), (), s32[]{:S(2)}) async-start(), calls=%async_computation.20 | async-start | bytes 2621440 | tf_op jit(solution)/shard_map/all_gather | solution.py:363
  540.0 73.2 %all-gather.19.cloned.1.call-start = ((), (), s32[]{:S(2)}) async-start(), calls=%async_computation.17 | async-start | bytes 2621440 | tf_op jit(solution)/shard_map/all_gather | solution.py:363
  572.3 417.9 %reduce-scatter.19.cloned.1.call-start = ((), (), s32[]{:S(2)}) async-start(), calls=%async_computation.18 | async-start | bytes 5242880 | tf_op jit(solution)/shard_map/reduce_scatter | solution.py:382
  769.4 220.8 %reduce-scatter.23.cloned.1.call-start = ((), (), s32[]{:S(2)}) async-start(), calls=%async_computation.21 | async-start | bytes 5242880 | tf_op jit(solution)/shard_map/reduce_scatter | solution.py:382
  889.0 145.4 %reduce-scatter.11.cloned.1.call-start = ((), (), s32[]{:S(2)}) async-start(), calls=%async_computation.11 | async-start | bytes 2621440 | tf_op jit(solution)/shard_map/reduce_scatter | solution.py:340
  896.8 514.6 %all-reduce.19.cloned.1.call-start = ((), (), s32[]{:S(2)}) async-start(), calls=%async_computation.24 | async-start | bytes 27787264 | tf_op jit(solution)/shard_map/psum | solution.py:395
  950.5 83.9 %copy-start.36 = (f32[256,1024]{1,0:T(8,128)S(1)}, f32[256,1024]{1,0:T(8,128)}, u32[]{:S(2)}) copy-start(f32[256,1024]{1,0:T(8,128)} %copy-done.34) | copy-start | bytes 3145732
  950.6 83.9 %copy-start.51 = (bf16[2,256,1024]{2,1,0:T(8,128)(2,1)S(1)}, bf16[2,256,1024]{2,1,0:T(8,128)(2,1)}, u32[]{:S(2)}) copy-start(bf16[2,256,1024]{2,1,0:T(8,128)(2,1)} %param.35) | copy-start | bytes 3145732
  950.6 83.9 %copy-start.152 = (f32[1024]{0:T(1024)S(1)}, f32[1024]{0:T(1024)}, u32[]{:S(2)}) copy-start(f32[1024]{0:T(1024)} %param.43) | copy-start | bytes 12292
  950.6 83.9 %copy-start.159 = (f32[256]{0:T(256)S(1)}, f32[256]{0:T(256)}, u32[]{:S(2)}) copy-start(f32[256]{0:T(256)} %copy-done.158) | copy-start | bytes 3076
  (252 other events, 1503.5 us)
Sparse Core Ops, SparseCore 0:
  12.7 25.2 all-gather.14
  40.1 22.5 all-gather.10
  136.1 44.5 reduce-scatter.12
  237.3 44.6 reduce-scatter.8
  286.8 22.5 all-gather.12
  311.4 22.5 all-gather.22
  347.9 44.4 reduce-scatter.16
  395.8 22.5 all-gather.16
  420.7 22.5 all-gather.24
  457.1 44.5 reduce-scatter.20
  504.8 31.4 reduce-scatter.14
  540.1 22.5 all-gather.20
  572.4 22.6 all-gather.18
  769.5 44.5 reduce-scatter.18
  889.1 44.5 reduce-scatter.22
  936.8 31.4 reduce-scatter.10
  974.7 436.7 all-reduce.18
where the time goes:
time: 1450 us; the launch traced here: 1440 us
  waiting for transfers between devices  581 us (40%)
  local copies, waits for them, and re-layouts  285 us (20%)
  matrix products  242 us (17%)
  other arithmetic  216 us (15%)
  blocking collectives  80.5 us (6%)
  between operations  21.1 us (1%)
    psum x1, waiting for transfers between devices, body(): lax.psum((grads[0], grads[1], grads[2], grads[3], grads[4], grads[5], gra...  370 us
    dot_general x16, matrix products, advance(): jnp.dot(lower, weighted.reshape(CTX, -1), precision=highest)  87.4 us
    reduce_scatter x2, waiting for transfers between devices, body(): lax.psum_scatter(grad_normed_two_part, 'mp', scatter_dimension=0, tiled=T...  47.2 us
    reduce_scatter x2, waiting for transfers between devices, body(): lax.psum_scatter(attn_part, 'mp', scatter_dimension=0, tiled=True)  44.7 us
    all_gather x2, waiting for transfers between devices, body(): normed_two_full = lax.all_gather(normed_two_low, 'mp', axis=0, tiled=True)  43.2 us
    while x312, local copies, waits for them, and re-layouts  42.1 us
    psum x1, blocking collectives, body(): gain_attn, gain_mlp = lax.psum((gain_first, gain_second), ('dp', 'mp'))  41.9 us
    psum x1, blocking collectives, body(): lax.psum((grads[0], grads[1], grads[2], grads[3], grads[4], grads[5], gra...  38.6 us
  transfers between devices with their start and end apart: 17, of which 10 were waited for; matrix products, arithmetic and copies ran while one was open for 36% of the time, Pallas kernels for 0%

commit v1 on v0

v1 whole, which is shorter than its diff:
```python
import functools
import math

import jax
import jax.numpy as jnp
from jax import lax
from jax.experimental import pallas as pl
from jax.experimental.pallas import tpu as pltpu
from jax.sharding import PartitionSpec as P

HD = 128
BLK = 512
CTX = 128
HEAD = BLK - CTX
NS = 16
EPS = 1e-05
SCALE = 1.0 / math.sqrt(HD)
SCALE2 = SCALE * math.log2(math.e)
NEG = -1e30
F32 = jnp.float32
BF16 = jnp.bfloat16

VMEM = pl.BlockSpec(memory_space=pltpu.VMEM)
SMEM = pl.BlockSpec(memory_space=pltpu.SMEM)
ANY = pl.BlockSpec(memory_space=pl.ANY)


def params(mib):
    return pltpu.CompilerParams(vmem_limit_bytes=mib << 20)


def cost(flops, nbytes):
    return pl.CostEstimate(flops=int(flops), bytes_accessed=int(nbytes), transcendentals=0)


def dot(a, b):
    return lax.dot_general(a, b, (((1,), (0,)), ((), ())), preferred_element_type=F32)


def dot_nt(a, b):
    return lax.dot_general(a, b, (((1,), (1,)), ((), ())), preferred_element_type=F32)


def dot_tn(a, b):
    return lax.dot_general(a, b, (((0,), (0,)), ((), ())), preferred_element_type=F32)


def shape(dims, kind):
    return jax.ShapeDtypeStruct(dims, kind)


def norm_one(tokens, gain, micro):
    rows, width = tokens.shape[1:]

    def kernel(x_ref, g_ref, o_ref):
        x = x_ref[0].astype(F32)
        scale = lax.rsqrt(jnp.mean(x * x, axis=-1, keepdims=True) + EPS)
        o_ref[...] = (x * scale * g_ref[...]).astype(BF16)

    return pl.pallas_call(
        kernel,
        grid=(1,),
        in_specs=[
            pl.BlockSpec((1, rows, width), lambda i: (micro, 0, 0)),
            pl.BlockSpec((1, width), lambda i: (0, 0)),
        ],
        out_specs=pl.BlockSpec((rows, width), lambda i: (0, 0)),
        out_shape=shape((rows, width), BF16),
        compiler_params=params(16),
        cost_estimate=cost(0, rows * width * 4),
    )(tokens, gain)


def first_of(rows, width):
    return pl.BlockSpec((1, rows, width), lambda i: (0, 0, 0))


def norm_two(tokens, part, sib, far, gain, micro):
    rows, width = tokens.shape[1:]

    def kernel(x_ref, p_ref, s_ref, r_ref, g_ref, mid_ref, o_ref):
        mid = (
            x_ref[0].astype(F32)
            + p_ref[0].astype(F32)
            + s_ref[0].astype(F32)
            + r_ref[...].astype(F32)
        )
        mid_ref[...] = mid
        scale = lax.rsqrt(jnp.mean(mid * mid, axis=-1, keepdims=True) + EPS)
        o_ref[...] = (mid * scale * g_ref[...]).astype(BF16)

    flat = pl.BlockSpec((rows, width), lambda i: (0, 0))
    return pl.pallas_call(
        kernel,
        grid=(1,),
        in_specs=[
            pl.BlockSpec((1, rows, width), lambda i: (micro, 0, 0)),
            first_of(rows, width),
            first_of(rows, width),
            flat,
            pl.BlockSpec((1, width), lambda i: (0, 0)),
        ],
        out_specs=[flat, flat],
        out_shape=[shape((rows, width), F32), shape((rows, width), BF16)],
        compiler_params=params(24),
        cost_estimate=cost(0, rows * width * 14),
    )(tokens, part, sib, far, gain)


def mix_out(middle, part, sib, far, prior, micro, count):
    rows, width = middle.shape

    def kernel(*refs):
        m_ref, p_ref, s_ref, r_ref = refs[:4]
        o_ref = refs[-1]
        branch = p_ref[0].astype(F32) + s_ref[0].astype(F32) + r_ref[...].astype(F32)
        o_ref[0] = (m_ref[...] + branch).astype(BF16)

    flat = pl.BlockSpec((rows, width), lambda i: (0, 0))
    specs = [flat, first_of(rows, width), first_of(rows, width), flat]
    args = [middle, part, sib, far]
    alias = {}
    if prior is not None:
        specs.append(ANY)
        args.append(prior)
        alias = {4: 0}
    return pl.pallas_call(
        kernel,
        grid=(1,),
        in_specs=specs,
        out_specs=pl.BlockSpec((1, rows, width), lambda i: (micro, 0, 0)),
        out_shape=shape((count, rows, width), BF16),
        input_output_aliases=alias,
        compiler_params=params(24),
        cost_estimate=cost(0, rows * width * 12),
    )(*args)


def norm_two_back(middle, part, sib, far, cotangent, gain, micro):
    rows, width = middle.shape

    def kernel(m_ref, p_ref, s_ref, r_ref, c_ref, g_ref, gm_ref, low_ref, gg_ref):
        mid = m_ref[...]
        grad = p_ref[0].astype(F32) + s_ref[0].astype(F32) + r_ref[...].astype(F32)
        scale = lax.rsqrt(jnp.mean(mid * mid, axis=-1, keepdims=True) + EPS)
        unit = mid * scale
        gg_ref[...] = jnp.sum(grad * unit, axis=0, keepdims=True)
        inner = grad * g_ref[...]
        pull = scale * (inner - unit * jnp.mean(inner * unit, axis=-1, keepdims=True))
        total = c_ref[0].astype(F32) + pull
        gm_ref[...] = total
        low_ref[...] = total.astype(BF16)

    flat = pl.BlockSpec((rows, width), lambda i: (0, 0))
    line = pl.BlockSpec((1, width), lambda i: (0, 0))
    return pl.pallas_call(
        kernel,
        grid=(1,),
        in_specs=[
            flat,
            first_of(rows, width),
            first_of(rows, width),
            flat,
            pl.BlockSpec((1, rows, width), lambda i: (micro, 0, 0)),
            line,
        ],
        out_specs=[flat, flat, line],
        out_shape=[
            shape((rows, width), F32),
            shape((rows, width), BF16),
            shape((1, width), F32),
        ],
        compiler_params=params(24),
        cost_estimate=cost(0, rows * width * 18),
    )(middle, part, sib, far, cotangent, gain)


def norm_one_back(tokens, part, sib, far, grad_middle, gain, prior, micro, count):
    rows, width = grad_middle.shape

    def kernel(*refs):
        x_ref, p_ref, s_ref, r_ref, gm_ref, g_ref = refs[:6]
        o_ref, gg_ref = refs[-2:]
        x = x_ref[0].astype(F32)
        grad = p_ref[0].astype(F32) + s_ref[0].astype(F32) + r_ref[...].astype(F32)
        scale = lax.rsqrt(jnp.mean(x * x, axis=-1, keepdims=True) + EPS)
        unit = x * scale
        gg_ref[...] = jnp.sum(grad * unit, axis=0, keepdims=True)
        inner = grad * g_ref[...]
        pull = scale * (inner - unit * jnp.mean(inner * unit, axis=-1, keepdims=True))
        o_ref[0] = gm_ref[...] + pull

    flat = pl.BlockSpec((rows, width), lambda i: (0, 0))
    line = pl.BlockSpec((1, width), lambda i: (0, 0))
    here = pl.BlockSpec((1, rows, width), lambda i: (micro, 0, 0))
    specs = [here, first_of(rows, width), first_of(rows, width), flat, flat, line]
    args = [tokens, part, sib, far, grad_middle, gain]
    alias = {}
    if prior is not None:
        specs.append(ANY)
        args.append(prior)
        alias = {6: 0}
    return pl.pallas_call(
        kernel,
        grid=(1,),
        in_specs=specs,
        out_specs=[here, line],
        out_shape=[shape((count, rows, width), F32), shape((1, width), F32)],
        input_output_aliases=alias,
        compiler_params=params(24),
        cost_estimate=cost(0, rows * width * 16),
    )(*args)


def add_second(part, sib):
    rows, width = part.shape[1:]

    def kernel(p_ref, s_ref, o_ref):
        o_ref[...] = (p_ref[0].astype(F32) + s_ref[0].astype(F32)).astype(BF16)

    second = pl.BlockSpec((1, rows, width), lambda i: (1, 0, 0))
    return pl.pallas_call(
        kernel,
        grid=(1,),
        in_specs=[second, second],
        out_specs=pl.BlockSpec((rows, width), lambda i: (0, 0)),
        out_shape=shape((rows, width), BF16),
        compiler_params=params(16),
        cost_estimate=cost(0, rows * width * 6),
    )(part, sib)


def flip(value, axis, bit):
    count = lax.axis_size(axis)
    return lax.ppermute(value, axis, [(i, i ^ bit) for i in range(count)])


def gather_mp(value):
    near = flip(value, "mp", 1)
    far = flip(value, "mp", 2)
    both = flip(far, "mp", 1)
    return (value, near, far, both)


def scatter_mp(keep, give):
    sib = flip(give, "mp", 1)
    far = flip(add_second(keep, sib), "mp", 2)
    return (keep, sib, far)


def triangle(upper):
    row = lax.broadcasted_iota(jnp.int32, (CTX, 2 * CTX), 0)
    col = lax.broadcasted_iota(jnp.int32, (CTX, 2 * CTX), 1) % CTX
    keep = (row <= col) if upper else (row >= col)
    return jnp.where(keep, 1.0, 0.0).astype(BF16)


def running(tri, values):
    high = values.astype(BF16)
    rest = (values - high.astype(F32)).astype(BF16)
    return dot(tri, jnp.concatenate([high, rest], axis=0))


def head_sums(u_ref, rate_ref, moment):
    width = rate_ref.shape[1]
    place = lax.broadcasted_iota(jnp.int32, (8, width), 0).astype(F32)
    sums, moments = [], []
    group = 4 if moment else 8
    for base in range(0, NS, group):
        rates = [rate_ref[n : n + 1, :] for n in range(base, base + group)]
        steps = [jnp.broadcast_to(jnp.exp(-8.0 * r), (8, width)) for r in rates]

        def body(chunk, carry):
            start = pl.multiple_of(chunk * 8, 8)
            rows = u_ref[pl.ds(start, 8), :]
            first = [acc * step + rows for acc, step in zip(carry[0], steps)]
            if not moment:
                return (first, carry[1])
            scaled = rows * (place + (chunk * 8 - HEAD).astype(F32))
            second = [acc * step + scaled for acc, step in zip(carry[1], steps)]
            return (first, second)

        zero = [jnp.zeros((8, width), F32) for _ in range(group)]
        first, second = lax.fori_loop(
            0, HEAD // 8, body, (zero, list(zero) if moment else []), unroll=4
        )
        for k, rate in enumerate(rates):
            last = jnp.exp(rate * (place - 8.0))
            sums.append(jnp.sum(first[k] * last, axis=0, keepdims=True))
            if moment:
                moments.append(jnp.sum(second[k] * last, axis=0, keepdims=True))
    return sums, moments


def state_forward(u_ref, rate_ref, in_ref, out_ref):
    width = rate_ref.shape[1]
    sums, _ = head_sums(u_ref, rate_ref, False)
    tail = u_ref[pl.ds(HEAD, CTX), :]
    time = lax.broadcasted_iota(jnp.int32, (CTX, width), 0).astype(F32)
    tri = triangle(False)
    total = jnp.zeros((CTX, width), F32)
    for n in range(NS):
        rate = rate_ref[n : n + 1, :]
        gain = in_ref[n : n + 1, :] * jnp.sqrt(1.0 - jnp.exp(-2.0 * rate))
        weight = gain * out_ref[n : n + 1, :]
        prefix = running(tri, jnp.exp(rate * time) * tail)
        total = total + weight * (jnp.exp(-rate * time) * (sums[n] + prefix))
    return total


def state_backward(grad, u_ref, du_ref, rate_ref, in_ref, out_ref, gs_ref):
    width = rate_ref.shape[1]
    sums, moments = head_sums(u_ref, rate_ref, True)
    tail = u_ref[pl.ds(HEAD, CTX), :]
    time = lax.broadcasted_iota(jnp.int32, (CTX, width), 0).astype(F32)
    place = lax.broadcasted_iota(jnp.int32, (8, width), 0).astype(F32)
    lower, upper = triangle(False), triangle(True)
    total = jnp.zeros((CTX, width), F32)
    starts = []
    for n in range(NS):
        rate = rate_ref[n : n + 1, :]
        root = jnp.sqrt(1.0 - jnp.exp(-2.0 * rate))
        enter = in_ref[n : n + 1, :]
        leave = out_ref[n : n + 1, :]
        gain = enter * root
        rising = jnp.exp(rate * time)
        driven = rising * tail
        states = sums[n] + running(lower, driven)
        seen = jnp.exp(-rate * time) * grad
        later = running(upper, seen)
        product = seen * states
        energy = jnp.sum(product, axis=0, keepdims=True)
        slope = jnp.sum(time * (product - driven * later), axis=0, keepdims=True)
        slope = slope - later[0:1] * moments[n]
        total = total + (gain * leave) * (rising * later)
        starts.append((gain * leave) * later[0:1])
        gs_ref[0, n : n + 1, :] = leave * (
            energy * enter * jnp.exp(-2.0 * rate) / root - gain * slope
        )
        gs_ref[1, n : n + 1, :] = leave * energy * root
        gs_ref[2, n : n + 1, :] = gain * energy
    du_ref[pl.ds(HEAD, CTX), :] = total
    group = 8
    for base in range(0, NS, group):
        rates = [rate_ref[n : n + 1, :] for n in range(base, base + group)]
        steps = [jnp.broadcast_to(jnp.exp(-8.0 * r), (8, width)) for r in rates]
        begin = [
            starts[base + k] * jnp.exp(rate * (place - 8.0)) for k, rate in enumerate(rates)
        ]

        def body(index, carry):
            start = pl.multiple_of(HEAD - 8 - index * 8, 8)
            value = functools.reduce(lambda a, b: a + b, carry)
            if base:
                value = value + du_ref[pl.ds(start, 8), :]
            du_ref[pl.ds(start, 8), :] = value
            return [c * step for c, step in zip(carry, steps)]

        lax.fori_loop(0, HEAD // 8, body, begin, unroll=4)


def layout_scalars(len_ref, micro):
    first, second = len_ref[micro, 0], len_ref[micro, 1]
    first_blocks = (first + (BLK - 1)) // BLK
    second_blocks = (second + (BLK - 1)) // BLK
    docs, valid = [], []
    for b in range(2):
        doc = jnp.where(b < first_blocks, 0, jnp.where(b < first_blocks + second_blocks, 1, 2))
        start = jnp.where(doc == 0, 0, first_blocks)
        extent = jnp.where(doc == 0, first, jnp.where(doc == 1, second, 0))
        docs.append(doc)
        valid.append(extent - (b - start) * BLK)
    return valid, docs[0] == docs[1]


def load_pieces(pieces, scratch, sems):
    for j, piece in enumerate(pieces):
        pltpu.make_async_copy(piece, scratch.at[j], sems.at[j]).start()


def wait_piece(pieces, scratch, sems, j):
    pltpu.make_async_copy(pieces[0], scratch.at[j], sems.at[j]).wait()


def attn_forward(pieces, in_w, rate, enter, leave, ctx_w, out_w, lengths, where, micro):
    rows, width = pieces[0].shape
    chans = out_w.shape[0]
    heads = chans // HD
    total = 4 * rows

    def kernel(
        me_ref, len_ref, n0, n1, n2, n3, w_ref, rate_ref, in_ref, out_ref, cw_ref, ow_ref,
        q_ref, k_ref, v_ref, u_ref, ctx_ref, ckv_ref, pr_ref, ho_ref, keep_ref, give_ref,
        xs, sems,
    ):
        me = me_ref[0]
        ns = (n0, n1, n2, n3)
        load_pieces(ns, xs, sems)

        def project(j, carry):
            wait_piece(ns, xs, sems, j)
            base = pl.multiple_of((me ^ j) * rows, rows)
            x = xs[j]
            q_ref[pl.ds(base, rows), :] = dot(x, w_ref[:, :chans]).astype(BF16)
            k_ref[pl.ds(base, rows), :] = dot(x, w_ref[:, chans : 2 * chans]).astype(BF16)
            v_ref[pl.ds(base, rows), :] = dot(x, w_ref[:, 2 * chans : 3 * chans]).astype(BF16)

            @pl.when(base < BLK)
            def _():
                u_ref[pl.ds(base, rows), :] = dot(x, w_ref[:, 3 * chans :])

            return carry

        lax.fori_loop(0, 4, project, 0)
        context = state_forward(u_ref, rate_ref, in_ref, out_ref).astype(BF16)
        ctx_ref[...] = context
        for h in range(heads):
            ckv_ref[h] = dot(context[:, h * HD : (h + 1) * HD], cw_ref[h]).astype(BF16)
        valid, linked = layout_scalars(len_ref, micro)
        for h in range(heads):
            lanes = slice(h * HD, (h + 1) * HD)
            for b in range(2):
                for half in range(2):
                    row0 = half * rows
                    keys = row0 + rows
                    q = q_ref[b * BLK + row0 : b * BLK + row0 + rows, lanes]
                    k = k_ref[b * BLK : b * BLK + keys, lanes]
                    v = v_ref[b * BLK : b * BLK + keys, lanes]
                    s = dot_nt(q, k) * SCALE2
                    row = lax.broadcasted_iota(jnp.int32, (rows, keys), 0) + row0
                    col = lax.broadcasted_iota(jnp.int32, (rows, keys), 1)
                    allowed = (col < jnp.minimum(row, valid[b])) | (col == row)
                    s = jnp.where(allowed, s, NEG)
                    peak = jnp.max(s, axis=-1, keepdims=True)
                    if b:
                        sc = dot_nt(q, ckv_ref[h, :, :HD]) * SCALE2
                        sc = jnp.where(linked, sc, NEG)
                        peak = jnp.maximum(peak, jnp.max(sc, axis=-1, keepdims=True))
                        ec = jnp.exp2(sc - peak)
                    e = jnp.exp2(s - peak)
                    norm = jnp.sum(e, axis=-1, keepdims=True)
                    if b:
                        norm = norm + jnp.sum(ec, axis=-1, keepdims=True)
                    inverse = 1.0 / norm
                    p = (e * inverse).astype(BF16)
                    pr_ref[h, b, row0 : row0 + rows, CTX : CTX + keys] = p
                    o = dot(p, v)
                    if b:
                        pc = (ec * inverse).astype(BF16)
                        pr_ref[h, b, row0 : row0 + rows, :CTX] = pc
                        o = o + dot(pc, ckv_ref[h, :, HD:])
                    ho_ref[me ^ (2 * b + half), :, lanes] = o.astype(BF16)
        for slot, j in enumerate((0, 2)):
            keep_ref[slot] = dot(ho_ref[j], ow_ref[...]).astype(BF16)
        for slot, j in enumerate((1, 3)):
            give_ref[slot] = dot(ho_ref[j], ow_ref[...]).astype(BF16)

    return pl.pallas_call(
        kernel,
        in_specs=[SMEM, SMEM] + [ANY] * 4 + [VMEM] * 6,
        out_specs=[VMEM] * 10,
        out_shape=[
            shape((total, chans), BF16),
            shape((total, chans), BF16),
            shape((total, chans), BF16),
            shape((BLK, chans), F32),
            shape((CTX, chans), BF16),
            shape((heads, CTX, 2 * HD), BF16),
            shape((heads, 2, BLK, BLK + CTX), BF16),
            shape((4, rows, chans), BF16),
            shape((2, rows, width), BF16),
            shape((2, rows, width), BF16),
        ],
        scratch_shapes=[pltpu.VMEM((4, rows, width), BF16), pltpu.SemaphoreType.DMA((4,))],
        compiler_params=params(48),
        cost_estimate=cost(12e9, 16e6),
    )(where, lengths, *pieces, in_w, rate, enter, leave, ctx_w, out_w)


def attn_backward(pieces, saved, in_w, rate, enter, leave, ctx_w, out_w, where):
    rows, width = pieces[0].shape
    chans = out_w.shape[0]
    heads = chans // HD
    total = 4 * rows
    q, k, v, u, ctx, ckv, probs = saved

    def kernel(
        me_ref, g0, g1, g2, g3, q_ref, k_ref, v_ref, u_ref, ctx_ref, ckv_ref, pr_ref,
        w_ref, rate_ref, in_ref, out_ref, cw_ref, ow_ref,
        gp_ref, keep_ref, give_ref, gcw_ref, gs_ref,
        gs, sems, dh, du, gctx,
    ):
        me = me_ref[0]
        gbs = (g0, g1, g2, g3)
        load_pieces(gbs, gs, sems)

        def heads_grad(j, carry):
            wait_piece(gbs, gs, sems, j)
            base = pl.multiple_of((me ^ j) * rows, rows)
            dh[pl.ds(base, rows), :] = dot_nt(gs[j], ow_ref[...]).astype(BF16)
            return carry

        lax.fori_loop(0, 4, heads_grad, 0)
        for h in range(heads):
            lanes = slice(h * HD, (h + 1) * HD)
            for b in range(2):
                grad_k = [None, None]
                grad_v = [None, None]
                grad_c = None
                grad_cv = None
                for half in (1, 0):
                    row0 = half * rows
                    keys = row0 + rows
                    spot = slice(b * BLK + row0, b * BLK + row0 + rows)
                    go = dh[spot, lanes]
                    qh = q_ref[spot, lanes]
                    kh = k_ref[b * BLK : b * BLK + keys, lanes]
                    vh = v_ref[b * BLK : b * BLK + keys, lanes]
                    p = pr_ref[h, b, row0 : row0 + rows, CTX : CTX + keys]
                    pf = p.astype(F32)
                    dp = dot_nt(go, vh)
                    delta = jnp.sum(dp * pf, axis=-1, keepdims=True)
                    if b:
                        pc = pr_ref[h, b, row0 : row0 + rows, :CTX]
                        pcf = pc.astype(F32)
                        dpc = dot_nt(go, ckv_ref[h, :, HD:])
                        delta = delta + jnp.sum(dpc * pcf, axis=-1, keepdims=True)
                        dsc = (pcf * (dpc - delta)).astype(BF16)
                    ds = (pf * (dp - delta)).astype(BF16)
                    dq = dot(ds, kh)
                    if b:
                        dq = dq + dot(dsc, ckv_ref[h, :, :HD])
                        one = dot_tn(dsc, qh)
                        two = dot_tn(pc, go)
                        grad_c = one if grad_c is None else grad_c + one
                        grad_cv = two if grad_cv is None else grad_cv + two
                    gp_ref[me ^ (2 * b + half), :, lanes] = (dq * SCALE).astype(BF16)
                    dk = dot_tn(ds, qh)
                    dv = dot_tn(p, go)
                    for part in range(half + 1):
                        cut = slice(part * rows, (part + 1) * rows)
                        if half:
                            grad_k[part] = dk[cut]
                            grad_v[part] = dv[cut]
                        else:
                            grad_k[0] = grad_k[0] + dk
                            grad_v[0] = grad_v[0] + dv
                for part in range(2):
                    slot = me ^ (2 * b + part)
                    gp_ref[slot, :, chans + h * HD : chans + (h + 1) * HD] = (
                        grad_k[part] * SCALE
                    ).astype(BF16)
                    gp_ref[slot, :, 2 * chans + h * HD : 2 * chans + (h + 1) * HD] = grad_v[
                        part
                    ].astype(BF16)
                if b:
                    low_c = (grad_c * SCALE).astype(BF16)
                    low_cv = grad_cv.astype(BF16)
                    ch = ctx_ref[:, lanes]
                    gcw_ref[h, :, :HD] = dot_tn(ch, low_c)
                    gcw_ref[h, :, HD:] = dot_tn(ch, low_cv)
                    gctx[:, lanes] = dot_nt(low_c, cw_ref[h, :, :HD]) + dot_nt(
                        low_cv, cw_ref[h, :, HD:]
                    )
        state_backward(gctx[...], u_ref, du, rate_ref, in_ref, out_ref, gs_ref)
        for b in range(2):
            for half in range(2):
                slot = me ^ (2 * b + half)
                if b:
                    gp_ref[slot, :, 3 * chans :] = jnp.zeros((rows, chans), BF16)
                else:
                    gp_ref[slot, :, 3 * chans :] = du[half * rows : (half + 1) * rows, :].astype(
                        BF16
                    )

        def back(slot, carry):
            keep_ref[slot] = dot_nt(gp_ref[2 * slot], w_ref[...]).astype(BF16)
            give_ref[slot] = dot_nt(gp_ref[2 * slot + 1], w_ref[...]).astype(BF16)
            return carry

        lax.fori_loop(0, 2, back, 0)

    return pl.pallas_call(
        kernel,
        in_specs=[SMEM] + [ANY] * 4 + [VMEM] * 13,
        out_specs=[VMEM] * 5,
        out_shape=[
            shape((4, rows, 4 * chans), BF16),
            shape((2, rows, width), BF16),
            shape((2, rows, width), BF16),
            shape((heads, CTX, 2 * HD), F32),
            shape((3, NS, chans), F32),
        ],
        scratch_shapes=[
            pltpu.VMEM((4, rows, width), BF16),
            pltpu.SemaphoreType.DMA((4,)),
            pltpu.VMEM((total, chans), BF16),
            pltpu.VMEM((BLK, chans), F32),
            pltpu.VMEM((CTX, chans), F32),
        ],
        compiler_params=params(48),
        cost_estimate=cost(20e9, 18e6),
    )(where, *pieces, q, k, v, u, ctx, ckv, probs, in_w, rate, enter, leave, ctx_w, out_w)


def feed(pieces, grads, up, down):
    rows, width = pieces[0].shape
    hidden = up.shape[1]
    root = math.sqrt(2.0 / math.pi)

    def kernel(
        n0, n1, n2, n3, c0, c1, c2, c3, up_ref, down_ref,
        hid_ref, gb_ref, fk_ref, fg_ref, gk_ref, gg_ref,
        xs, cs, xsem, csem,
    ):
        i = pl.program_id(0)
        order = (0, 2, 1, 3)
        ns, cots = (n0, n1, n2, n3), (c0, c1, c2, c3)

        @pl.when(i == 0)
        def _():
            for step, j in enumerate(order):
                pltpu.make_async_copy(ns[j], xs.at[step], xsem.at[step]).start()
                pltpu.make_async_copy(cots[j], cs.at[step], csem.at[step]).start()

        wait_piece(ns, xs, xsem, i)
        wait_piece(cots, cs, csem, i)
        before = dot(xs[i], up_ref[...])
        square = before * before
        t = jnp.tanh(root * (before * (1.0 + 0.044715 * square)))
        half = 0.5 + 0.5 * t
        hid = (before * half).astype(BF16)
        hid_ref[0] = hid
        slope = half + (0.5 * root) * before * (1.0 - t * t) * (1.0 + 0.134145 * square)
        branch = dot(hid, down_ref[...]).astype(BF16)
        gh = dot_nt(cs[i], down_ref[...])
        gb = (gh * slope).astype(BF16)
        gb_ref[0] = gb
        gn = dot_nt(gb, up_ref[...]).astype(BF16)

        @pl.when(i < 2)
        def _():
            fk_ref[0] = branch
            gk_ref[0] = gn

        @pl.when(i >= 2)
        def _():
            fg_ref[0] = branch
            gg_ref[0] = gn

    whole = pl.BlockSpec(memory_space=pltpu.VMEM)
    low = pl.BlockSpec((1, rows, width), lambda i: (jnp.minimum(i, 1), 0, 0))
    high = pl.BlockSpec((1, rows, width), lambda i: (jnp.maximum(i - 2, 0), 0, 0))
    at = pl.BlockSpec((1, rows, hidden), lambda i: (i, 0, 0))
    return pl.pallas_call(
        kernel,
        grid=(4,),
        in_specs=[ANY] * 8 + [whole] * 2,
        out_specs=[at, at, low, high, low, high],
        out_shape=[
            shape((4, rows, hidden), BF16),
            shape((4, rows, hidden), BF16),
        ]
        + [shape((2, rows, width), BF16)] * 4,
        scratch_shapes=[
            pltpu.VMEM((4, rows, width), BF16),
            pltpu.VMEM((4, rows, width), BF16),
            pltpu.SemaphoreType.DMA((4,)),
            pltpu.SemaphoreType.DMA((4,)),
        ],
        compiler_params=params(40),
        cost_estimate=cost(30e9, 16e6),
    )(*pieces, *grads, up, down)


def weight_grad(lefts, rights, left_order, right_order, flag):
    def expand(values, order):
        refs, picks = [], []
        for value in values:
            if isinstance(value, tuple):
                for j in order:
                    picks.append((len(refs) + j, None))
                refs.extend(value)
            else:
                for j in order:
                    picks.append((len(refs), j))
                refs.append(value)
        return refs, picks

    lrefs, lpicks = expand(lefts, left_order)
    rrefs, rpicks = expand(rights, right_order)
    count = len(lpicks)
    rows = lrefs[0].shape[-2]
    m, n = lrefs[0].shape[-1], rrefs[0].shape[-1]
    nl, nr = len(lrefs), len(rrefs)

    def kernel(*refs):
        flag_ref = refs[0]
        ls, rs = refs[1 : 1 + nl], refs[1 + nl : 1 + nl + nr]
        keep_ref, give_ref, acc, lbuf, rbuf, lsem, rsem = refs[1 + nl + nr :]
        i = pl.program_id(0)

        def fetch(step):
            lk, lj = lpicks[step]
            rk, rj = rpicks[step]
            lsrc = ls[lk] if lj is None else ls[lk].at[lj]
            rsrc = rs[rk] if rj is None else rs[rk].at[rj]
            pltpu.make_async_copy(lsrc, lbuf.at[step], lsem.at[step]).start()
            pltpu.make_async_copy(rsrc, rbuf.at[step], rsem.at[step]).start()

        @pl.when(i == 0)
        def _():
            for step in range(count):
                fetch(step)

        lany = ls[0] if lpicks[0][1] is None else ls[0].at[0]
        rany = rs[0] if rpicks[0][1] is None else rs[0].at[0]
        pltpu.make_async_copy(lany, lbuf.at[i], lsem.at[i]).wait()
        pltpu.make_async_copy(rany, rbuf.at[i], rsem.at[i]).wait()
        product = dot_tn(lbuf[i], rbuf[i])

        @pl.when(i == 0)
        def _():
            acc[...] = product

        @pl.when(i > 0)
        def _():
            acc[...] += product

        @pl.when(i == count - 1)
        def _():
            mine = flag_ref[1]
            keep_ref[...] = acc[pl.ds(pl.multiple_of(mine * (m // 2), m // 2), m // 2), :].astype(
                BF16
            )
            give_ref[...] = acc[
                pl.ds(pl.multiple_of((1 - mine) * (m // 2), m // 2), m // 2), :
            ].astype(BF16)

    full = pl.BlockSpec((m // 2, n), lambda i: (0, 0))
    return pl.pallas_call(
        kernel,
        grid=(count,),
        in_specs=[SMEM] + [ANY] * (nl + nr),
        out_specs=[full, full],
        out_shape=[shape((m // 2, n), BF16)] * 2,
        scratch_shapes=[
            pltpu.VMEM((m, n), F32),
            pltpu.VMEM((count, rows, m), BF16),
            pltpu.VMEM((count, rows, n), BF16),
            pltpu.SemaphoreType.DMA((count,)),
            pltpu.SemaphoreType.DMA((count,)),
        ],
        compiler_params=params(40),
        cost_estimate=cost(2 * count * rows * m * n * 2, 2 * count * rows * (m + n)),
    )(flag, *lrefs, *rrefs)


def split_sum(keep, got, flag, nz):
    rows, width = keep.shape
    piece = rows // nz

    def kernel(flag_ref, a_ref, b_ref, *outs):
        own = flag_ref[2]
        for k in range(nz):
            at = pl.ds(pl.multiple_of((own ^ k) * piece, piece), piece)
            outs[k][...] = (a_ref[at, :].astype(F32) + b_ref[at, :].astype(F32)).astype(BF16)

    return pl.pallas_call(
        kernel,
        in_specs=[SMEM, VMEM, VMEM],
        out_specs=[VMEM] * nz,
        out_shape=[shape((piece, width), BF16)] * nz,
        compiler_params=params(16),
        cost_estimate=cost(0, rows * width * 6),
    )(flag, keep, got)


def add_all(values):
    rows, width = values[0].shape

    def kernel(*refs):
        total = refs[0][...].astype(F32)
        for ref in refs[1:-1]:
            total = total + ref[...].astype(F32)
        refs[-1][...] = total.astype(BF16)

    return pl.pallas_call(
        kernel,
        in_specs=[VMEM] * len(values),
        out_specs=VMEM,
        out_shape=shape((rows, width), BF16),
        compiler_params=params(16),
        cost_estimate=cost(0, rows * width * 2 * len(values)),
    )(*values)


def join(values, flag):
    piece, width = values[0].shape
    nz = len(values)

    def kernel(flag_ref, *refs):
        own = flag_ref[2]
        for k in range(nz):
            at = pl.ds(pl.multiple_of((own ^ k) * piece, piece), piece)
            refs[-1][at, :] = refs[k][...]

    return pl.pallas_call(
        kernel,
        in_specs=[SMEM] + [VMEM] * nz,
        out_specs=VMEM,
        out_shape=shape((nz * piece, width), BF16),
        compiler_params=params(16),
        cost_estimate=cost(0, nz * piece * width * 4),
    )(flag, *values)


def unpack(half, other, flag):
    rows, width = half.shape

    def kernel(flag_ref, a_ref, b_ref, o_ref):
        mine = flag_ref[1]
        o_ref[pl.ds(pl.multiple_of(mine * rows, rows), rows), :] = a_ref[...].astype(F32)
        o_ref[pl.ds(pl.multiple_of((1 - mine) * rows, rows), rows), :] = b_ref[...].astype(F32)

    return pl.pallas_call(
        kernel,
        in_specs=[SMEM, VMEM, VMEM],
        out_specs=VMEM,
        out_shape=shape((2 * rows, width), F32),
        compiler_params=params(24),
        cost_estimate=cost(0, rows * width * 12),
    )(flag, half, other)


def reduce_dp(keep, give, flag, nz):
    got = flip(give, "dp", 1)
    pieces = split_sum(keep, got, flag, nz)
    parts = [pieces[0]] + [flip(pieces[k], "dp", 2 * k) for k in range(1, nz)]
    own = add_all(parts)
    half = join([own] + [flip(own, "dp", 2 * k) for k in range(1, nz)], flag)
    return unpack(half, flip(half, "dp", 1), flag)


def body(
    tokens,
    lengths,
    cotangent,
    attn_gain,
    in_weights,
    ssm_rate,
    ssm_input,
    ssm_output,
    ctx_weights,
    out_weights,
    mlp_gain,
    up_weights,
    down_weights,
):
    count, rows, width = tokens.shape
    chans = out_weights.shape[0]
    nz = lax.axis_size("dp") // 2
    dp = lax.axis_index("dp")
    flag = jnp.stack([lax.axis_index("mp"), dp % 2, dp // 2]).astype(jnp.int32)
    lens = lengths[0]
    flat_in = in_weights.reshape(width, 4 * chans)
    gain_one = attn_gain.reshape(1, width)
    gain_two = mlp_gain.reshape(1, width)
    ssm = (ssm_rate, ssm_input, ssm_output)
    micros = range(count)

    normed = [gather_mp(norm_one(tokens, gain_one, m)) for m in micros]
    cots = [gather_mp(cotangent[m]) for m in micros]
    saved, heads_out, middles, normed_two = [], [], [], []
    for m in micros:
        *kept, ho, keep, give = attn_forward(
            normed[m], flat_in, *ssm, ctx_weights, out_weights, lens, flag, m
        )
        saved.append(kept)
        heads_out.append(ho)
        middle, low = norm_two(tokens, *scatter_mp(keep, give), gain_two, m)
        middles.append(middle)
        normed_two.append(gather_mp(low))
    hidden, grad_before, grad_mid, branch, gain_two_parts = [], [], [], [], []
    mixed = None
    for m in micros:
        hid, gb, fk, fg, gk, gg = feed(normed_two[m], cots[m], up_weights, down_weights)
        hidden.append(hid)
        grad_before.append(gb)
        gm, low, part = norm_two_back(
            middles[m], *scatter_mp(gk, gg), cotangent, gain_two, m
        )
        grad_mid.append(gm)
        gain_two_parts.append(part)
        branch.append(gather_mp(low))
        mixed = mix_out(middles[m], *scatter_mp(fk, fg), mixed, m, count)
    natural, mixed_order = (0, 1, 2, 3), (0, 2, 1, 3)
    up_parts = weight_grad(normed_two, grad_before, mixed_order, natural, flag)
    grad_up = reduce_dp(*up_parts, flag, nz)
    down_parts = weight_grad(hidden, cots, natural, mixed_order, flag)
    grad_down = reduce_dp(*down_parts, flag, nz)
    grad_proj, small, gain_one_parts = [], [], []
    grad_tokens = None
    for m in micros:
        gp, keep, give, gcw, gs = attn_backward(
            branch[m], saved[m], flat_in, *ssm, ctx_weights, out_weights, flag
        )
        grad_proj.append(gp)
        small.append((gcw, gs))
        grad_tokens, part = norm_one_back(
            tokens, *scatter_mp(keep, give), grad_mid[m], gain_one, grad_tokens, m, count
        )
        gain_one_parts.append(part)
    in_parts = weight_grad(normed, grad_proj, natural, natural, flag)
    grad_in = reduce_dp(*in_parts, flag, nz)
    out_parts = weight_grad(heads_out, branch, natural, natural, flag)
    grad_out = reduce_dp(*out_parts, flag, nz)

    gcw = functools.reduce(lambda a, b: a + b, [s[0] for s in small])
    gs = functools.reduce(lambda a, b: a + b, [s[1] for s in small])
    gains = jnp.concatenate(
        [
            functools.reduce(lambda a, b: a + b, gain_one_parts),
            functools.reduce(lambda a, b: a + b, gain_two_parts),
        ]
    )
    gains = gains + flip(gains, "mp", 1)
    gains = gains + flip(gains, "mp", 2)
    packed = jnp.concatenate(
        [gcw.reshape(-1, width), gs.reshape(-1, width), gains], axis=0
    ).astype(BF16)
    need = packed.shape[0]
    unit = 2 * nz * 16
    padded = jnp.pad(packed, ((0, -need % unit), (0, 0)))
    two = padded.reshape(2, padded.shape[0] // 2, width)
    pack = reduce_dp(
        lax.dynamic_index_in_dim(two, dp % 2, keepdims=False),
        lax.dynamic_index_in_dim(two, 1 - dp % 2, keepdims=False),
        flag,
        nz,
    )
    n_ctx = gcw.size // width
    n_ssm = gs.size // width
    grad_ctx = pack[:n_ctx].reshape(gcw.shape)
    grad_ssm = pack[n_ctx : n_ctx + n_ssm].reshape(gs.shape)
    return (
        mixed,
        grad_tokens,
        pack[n_ctx + n_ssm],
        grad_in.reshape(in_weights.shape),
        grad_ssm[0],
        grad_ssm[1],
        grad_ssm[2],
        grad_ctx,
        grad_out,
        pack[n_ctx + n_ssm + 1],
        grad_up,
        grad_down,
    )


def solution(mesh):
    rows = P(None, ("dp", "mp"), None)
    return jax.shard_map(
        body,
        mesh=mesh,
        in_specs=(
            rows,
            P("dp", None, None),
            rows,
            P(),
            P(None, None, "mp"),
            P(None, "mp"),
            P(None, "mp"),
            P(None, "mp"),
            P("mp", None, None),
            P("mp", None),
            P(),
            P(None, "mp"),
            P("mp", None),
        ),
        out_specs=(
            rows,
            rows,
            P(),
            P(None, None, "mp"),
            P(None, "mp"),
            P(None, "mp"),
            P(None, "mp"),
            P("mp", None, None),
            P("mp", None),
            P(),
            P(None, "mp"),
            P("mp", None),
        ),
        check_vma=False,
    )
```

time: 1450 us -> 520 us (0.36)
  waiting for transfers between devices: 581 us -> 192 us
  matrix products: 242 us -> 0 us
  local copies, waits for them, and re-layouts: 285 us -> 57.8 us
  other arithmetic: 216 us -> 2.26 us
  Pallas kernels: 0 us -> 165 us
  starting transfers between devices: 1.97 us -> 93.4 us
  blocking collectives: 80.5 us -> 0 us
  between operations: 21.1 us -> 2.48 us
    psum x1 -> x0, waiting for transfers between devices: 370 us -> none  [body(): lax.psum((grads[0], grads[1], grads[2], grads[3], grads[4], grads[5], gra...]
    dot_general x108 -> x0, matrix products: 242 us -> none  [the longest x16 87.4 us: advance(): jnp.dot(lower, weighted.reshape(CTX, -1), precision=highest)]
    ppermute x0 -> x82, waiting for transfers between devices: none -> 192 us  [flip(): return lax.ppermute(value, axis, [(i, i ^ bit) for i in range(count)])]
    pallas_call x0 -> x48, Pallas kernels: none -> 165 us  [the longest x4 41.8 us: weight_grad(): pl.pallas_call(kernel, grid=(count,), in_specs=[SMEM] + [ANY] * (nl + nr)...]
    reduce_scatter x8 -> x0, waiting for transfers between devices: 124 us -> none  [the longest x2 47.2 us: body(): lax.psum_scatter(grad_normed_two_part, 'mp', scatter_dimension=0, tiled=T...]
    ppermute x0 -> x82, starting transfers between devices: none -> 93.4 us  [flip(): return lax.ppermute(value, axis, [(i, i ^ bit) for i in range(count)])]
    all_gather x8 -> x0, waiting for transfers between devices: 84.4 us -> none  [the longest x2 43.2 us: body(): normed_two_full = lax.all_gather(normed_two_low, 'mp', axis=0, tiled=True)]
    psum x2 -> x0, blocking collectives: 80.5 us -> none  [the longest x1 41.9 us: body(): gain_attn, gain_mlp = lax.psum((gain_first, gain_second), ('dp', 'mp'))]
  transfers between devices with their start and end apart: 17 -> 82, of which waited for: 10 -> 28; matrix products, arithmetic and copies ran while one was open for 36% -> 2% of each run, Pallas kernels for 0% -> 32%
where the time goes in v1:
time: 520 us; the launch traced here: 513 us
  waiting for transfers between devices  192 us (37%)
  Pallas kernels  165 us (32%)
  starting transfers between devices  93.4 us (18%)
  local copies, waits for them, and re-layouts  57.8 us (11%)
    ppermute x82, waiting for transfers between devices, flip(): return lax.ppermute(value, axis, [(i, i ^ bit) for i in range(count)])  192 us
    ppermute x82, starting transfers between devices, flip(): return lax.ppermute(value, axis, [(i, i ^ bit) for i in range(count)])  93.4 us
    unnamed x295, local copies, waits for them, and re-layouts  48.1 us
    pallas_call x4, Pallas kernels, weight_grad(): pl.pallas_call(kernel, grid=(count,), in_specs=[SMEM] + [ANY] * (nl + nr)...  41.8 us
    pallas_call x2, Pallas kernels, attn_backward(): pl.pallas_call(kernel, in_specs=[SMEM] + [ANY] * 4 + [VMEM] * 13, out_spe...  32 us
    pallas_call x2, Pallas kernels, feed(): pl.pallas_call(kernel, grid=(4,), in_specs=[ANY] * 8 + [whole] * 2, out_s...  28.1 us
    pallas_call x2, Pallas kernels, attn_forward(): pl.pallas_call(kernel, in_specs=[SMEM, SMEM] + [ANY] * 4 + [VMEM] * 6, ou...  25.7 us
  transfers between devices with their start and end apart: 82, of which 28 were waited for; matrix products, arithmetic and copies ran while one was open for 2% of the time, Pallas kernels for 32%

profile of v1, /device:TPU:0, one launch (start us, length us, event | category | flops | bytes accessed | tf_op | source)
XLA Modules:
  0.0 513.2 jit_solution(15671479816311275123)
XLA Ops:
  6.2 12.4 %collective-permute-done.1.n2.refs_7_ = bf16[256,1024]{1,0:T(8,128)(2,1)S(1)} collective-permute-done((bf16[256,1024]{1,0:T(8,128)(2,1)S(1)}, bf16[256,1024]{1,0:T(8,128)(2,1)S(1)}, u32[]{:S(2)}, u32[]{:S(2)}) %collective-permute-start.1) | collective-permute-done | bytes 524320 | tf_op jit(solution)/shard_map/ppermute | solution.py:235
  29.1 12.5 %shard_map.221 = (bf16[1024,256]{1,0:T(8,128)(2,1)S(1)}, bf16[1024,256]{1,0:T(8,128)(2,1)S(1)}, bf16[1024,256]{1,0:T(8,128)(2,1)S(1)}, f32[512,256]{1,0:T(8,128)...) custom-call(s32[3]{0:T(128)S(1)} %pad_add_fusion.me_ref.flag_ref.ref, ...), custom_call_target="tpu_custom_call" | custom-call | flops 12000000000 | bytes 16000000 | tf_op jit(solution)/shard_map/pallas_call | solution.py:458
  45.6 13.2 %shard_map.227 = (bf16[1024,256]{1,0:T(8,128)(2,1)S(1)}, bf16[1024,256]{1,0:T(8,128)(2,1)S(1)}, bf16[1024,256]{1,0:T(8,128)(2,1)S(1)}, f32[512,256]{1,0:T(8,128)...) custom-call(s32[3]{0:T(128)S(1)} %pad_add_fusion.me_ref.flag_ref.ref, ...), custom_call_target="tpu_custom_call" | custom-call | flops 12000000000 | bytes 16000000 | tf_op jit(solution)/shard_map/pallas_call | solution.py:458
  66.4 10.2 %collective-permute-done.4.r_ref = bf16[256,1024]{1,0:T(8,128)(2,1)S(1)} collective-permute-done((bf16[256,1024]{1,0:T(8,128)(2,1)S(1)}, bf16[256,1024]{1,0:T(8,128)(2,1)S(1)}, u32[]{:S(2)}, u32[]{:S(2)}) %collective-permute-start.4) | collective-permute-done | bytes 524320 | tf_op jit(solution)/shard_map/ppermute | solution.py:235
  79.2 8.6 %collective-permute-done.9.c2.refs_9_ = bf16[256,1024]{1,0:T(8,128)(2,1)S(1)} collective-permute-done((bf16[256,1024]{1,0:T(8,128)(2,1)S(1)}, bf16[256,1024]{1,0:T(8,128)(2,1)S(1)}, u32[]{:S(2)}, u32[]{:S(2)}) %collective-permute-start.9) | collective-permute-done | bytes 524320 | tf_op jit(solution)/shard_map/ppermute | solution.py:235
  87.8 11.2 %collective-permute-done.17.r_ref = bf16[256,1024]{1,0:T(8,128)(2,1)S(1)} collective-permute-done((bf16[256,1024]{1,0:T(8,128)(2,1)S(1)}, bf16[256,1024]{1,0:T(8,128)(2,1)S(1)}, u32[]{:S(2)}, u32[]{:S(2)}) %collective-permute-start.17) | collective-permute-done | bytes 524320 | tf_op jit(solution)/shard_map/ppermute | solution.py:235
  101.6 8.7 %collective-permute-done.6.n2.refs_7_ = bf16[256,1024]{1,0:T(8,128)(2,1)S(1)} collective-permute-done((bf16[256,1024]{1,0:T(8,128)(2,1)S(1)}, bf16[256,1024]{1,0:T(8,128)(2,1)S(1)}, u32[]{:S(2)}, u32[]{:S(2)}) %collective-permute-start.6) | collective-permute-done | bytes 524320 | tf_op jit(solution)/shard_map/ppermute | solution.py:235
  110.3 11.2 %collective-permute-done.22.c2.refs_5_ = bf16[256,1024]{1,0:T(8,128)(2,1)S(1)} collective-permute-done((bf16[256,1024]{1,0:T(8,128)(2,1)S(1)}, bf16[256,1024]{1,0:T(8,128)(2,1)S(1)}, u32[]{:S(2)}, u32[]{:S(2)}) %collective-permute-start.22) | collective-permute-done | bytes 524320 | tf_op jit(solution)/shard_map/ppermute | solution.py:235
  122.1 10.4 %collective-permute-done.19.n2.refs_3_ = bf16[256,1024]{1,0:T(8,128)(2,1)S(1)} collective-permute-done((bf16[256,1024]{1,0:T(8,128)(2,1)S(1)}, bf16[256,1024]{1,0:T(8,128)(2,1)S(1)}, u32[]{:S(2)}, u32[]{:S(2)}) %collective-permute-start.19) | collective-permute-done | bytes 524320 | tf_op jit(solution)/shard_map/ppermute | solution.py:235
  132.5 13.8 %shard_map.224 = (bf16[4,256,1024]{2,1,0:T(8,128)(2,1)S(1)}, bf16[4,256,1024]{2,1,0:T(8,128)(2,1)S(1)}, bf16[2,256,1024]{2,1,0:T(8,128)(2,1)S(1)}, bf16[2,256,10...) custom-call(bf16[256,1024]{1,0:T(8,128)(2,1)S(1)} %get-tuple-element.99.n0.refs_5_, ...), custom_call_target="tpu_custom_call" | custom-call | flops 30000001024 | bytes 16000000 | tf_op jit(solution)/shard_map/pallas_call | solution.py:655
  150.6 14.3 %shard_map.230 = (bf16[4,256,1024]{2,1,0:T(8,128)(2,1)S(1)}, bf16[4,256,1024]{2,1,0:T(8,128)(2,1)S(1)}, bf16[2,256,1024]{2,1,0:T(8,128)(2,1)S(1)}, bf16[2,256,10...) custom-call(bf16[256,1024]{1,0:T(8,128)(2,1)S(1)} %get-tuple-element.105.n0.refs_1_, ...), custom_call_target="tpu_custom_call" | custom-call | flops 30000001024 | bytes 16000000 | tf_op jit(solution)/shard_map/pallas_call | solution.py:655
  170.3 11.7 %shard_map.258 = (bf16[512,1024]{1,0:T(8,128)(2,1)S(1)}, bf16[512,1024]{1,0:T(8,128)(2,1)}) custom-call(s32[3]{0:T(128)S(1)} %pad_add_fusion.me_ref.flag_ref.refs_0_, bf16[256,1024]{1,0:T(8,128)(2,1)S(1)} %copy-done.100, bf16[256,1024]{1,0:T(8,128)(2,1)S(1)} %collective-permute-done.18.n1.refs_2_, bf16[256,1024]{1,0:T(8,128)(2,1)S(1)} %collective-permute-done.19.n2.refs_3_, ...), custom_call_target="tpu_custom_call" | custom-call | flops 8589934592 | bytes 8388608 | tf_op jit(solution)/shard_map/pallas_call | solution.py:741
  189.8 11.7 %shard_map.263 = (bf16[512,1024]{1,0:T(8,128)(2,1)S(1)}, bf16[512,1024]{1,0:T(8,128)(2,1)}) custom-call(s32[3]{0:T(128)S(1)} %pad_add_fusion.me_ref.flag_ref.refs_0_, bf16[4,256,1024]{2,1,0:T(8,128)(2,1)S(1)} %copy-done.119, bf16[4,256,1024]{2,1,0:T(8,128)(2,1)S(1)} %copy-done.116, bf16[256,1024]{1,0:T(8,128)(2,1)S(1)} %get-tuple-element.180.c0.refs_3_, ...), custom_call_target="tpu_custom_call" | custom-call | flops 8589934592 | bytes 8388608 | tf_op jit(solution)/shard_map/pallas_call | solution.py:741
  205.1 12.1 %collective-permute-done.34.r_ref = bf16[256,1024]{1,0:T(8,128)(2,1)S(1)} collective-permute-done((bf16[256,1024]{1,0:T(8,128)(2,1)S(1)}, bf16[256,1024]{1,0:T(8,128)(2,1)S(1)}, u32[]{:S(2)}, u32[]{:S(2)}) %collective-permute-start.34) | collective-permute-done | bytes 524320 | tf_op jit(solution)/shard_map/ppermute | solution.py:235
  218.7 9.7 %collective-permute-done.29.g2.refs_9_ = bf16[256,1024]{1,0:T(8,128)(2,1)S(1)} collective-permute-done((bf16[256,1024]{1,0:T(8,128)(2,1)S(1)}, bf16[256,1024]{1,0:T(8,128)(2,1)S(1)}, u32[]{:S(2)}, u32[]{:S(2)}) %collective-permute-start.29) | collective-permute-done | bytes 524320 | tf_op jit(solution)/shard_map/ppermute | solution.py:235
  241.6 15.8 %shard_map.236 = (bf16[4,256,1024]{2,1,0:T(8,128)(2,1)}, bf16[2,256,1024]{2,1,0:T(8,128)(2,1)}, bf16[2,256,1024]{2,1,0:T(8,128)(2,1)}, f32[2,128,256]{2,1,0:T(8,128)S(1)}, f32[3,16,256]{2,1,0:T(8,128)S(1)}) custom-call(s32[3]{0:T(128)S(1)} %pad_add_fusion.me_ref.flag_ref.refs_0_, bf16[256,1024]{1,0:T(8,128)(2,1)S(1)} %get-tuple-element.110.g0.refs_7_, ...), custom_call_target="tpu_custom_call" | custom-call | flops 20000000000 | bytes 18000000 | tf_op jit(solution)/shard_map/pallas_call | solution.py:583
  267.1 16.1 %shard_map.240 = (bf16[4,256,1024]{2,1,0:T(8,128)(2,1)}, bf16[2,256,1024]{2,1,0:T(8,128)(2,1)}, bf16[2,256,1024]{2,1,0:T(8,128)(2,1)}, f32[2,128,256]{2,1,0:T(8,128)S(1)}, f32[3,16,256]{2,1,0:T(8,128)S(1)}) custom-call(s32[3]{0:T(128)S(1)} %pad_add_fusion.me_ref.flag_ref.refs_0_, bf16[256,1024]{1,0:T(8,128)(2,1)S(1)} %copy-done.83, ...), custom_call_target="tpu_custom_call" | custom-call | flops 20000000000 | bytes 18000000 | tf_op jit(solution)/shard_map/pallas_call | solution.py:583
  291.4 11.6 %shard_map.248 = (bf16[512,1024]{1,0:T(8,128)(2,1)S(1)}, bf16[512,1024]{1,0:T(8,128)(2,1)}) custom-call(s32[3]{0:T(128)S(1)} %pad_add_fusion.me_ref.flag_ref.refs_0_, bf16[256,1024]{1,0:T(8,128)(2,1)S(1)} %copy-done.36, bf16[256,1024]{1,0:T(8,128)(2,1)} %collective-permute-done.13.n1.refs_2_, bf16[256,1024]{1,0:T(8,128)(2,1)S(1)} %copy-done.69, ...), custom_call_target="tpu_custom_call" | custom-call | flops 8589934592 | bytes 8388608 | tf_op jit(solution)/shard_map/pallas_call | solution.py:741
  316.3 11.8 %collective-permute-done.71.refs_2_ = bf16[128,1024]{1,0:T(8,128)(2,1)S(1)} collective-permute-done((bf16[128,1024]{1,0:T(8,128)(2,1)S(1)}, bf16[128,1024]{1,0:T(8,128)(2,1)S(1)}, u32[]{:S(2)}, u32[]{:S(2)}) %collective-permute-start.71) | collective-permute-done | bytes 262176 | tf_op jit(solution)/shard_map/ppermute | solution.py:235
  339.8 10.7 %collective-permute-done.79.refs_2_ = bf16[128,1024]{1,0:T(8,128)(2,1)S(1)} collective-permute-done((bf16[128,1024]{1,0:T(8,128)(2,1)S(1)}, bf16[128,1024]{1,0:T(8,128)(2,1)S(1)}, u32[]{:S(2)}, u32[]{:S(2)}) %collective-permute-start.79) | collective-permute-done | bytes 262176 | tf_op jit(solution)/shard_map/ppermute | solution.py:235
  351.3 6.8 %shard_map.253 = (bf16[128,1024]{1,0:T(8,128)(2,1)S(1)}, bf16[128,1024]{1,0:T(8,128)(2,1)}) custom-call(s32[3]{0:T(128)S(1)} %pad_add_fusion.me_ref.flag_ref.refs_0_, bf16[4,256,256]{2,1,0:T(8,128)(2,1)S(1)} %copy-done.113, bf16[4,256,256]{2,1,0:T(8,128)(2,1)S(1)} %copy-done.111, bf16[256,1024]{1,0:T(8,128)(2,1)S(1)} %copy-done.83, ...), custom_call_target="tpu_custom_call" | custom-call | flops 2147483648 | bytes 5242880 | tf_op jit(solution)/shard_map/pallas_call | solution.py:741
  379.4 11.1 %collective-permute-done.52.refs_2_ = bf16[128,1024]{1,0:T(8,128)(2,1)S(1)} collective-permute-done((bf16[128,1024]{1,0:T(8,128)(2,1)S(1)}, bf16[128,1024]{1,0:T(8,128)(2,1)S(1)}, u32[]{:S(2)}, u32[]{:S(2)}) %collective-permute-start.52) | collective-permute-done | bytes 262176 | tf_op jit(solution)/shard_map/ppermute | solution.py:235
  415.9 9.3 %collective-permute-done.55.refs_2_ = bf16[128,1024]{1,0:T(8,128)(2,1)S(1)} collective-permute-done((bf16[128,1024]{1,0:T(8,128)(2,1)S(1)}, bf16[128,1024]{1,0:T(8,128)(2,1)S(1)}, u32[]{:S(2)}, u32[]{:S(2)}) %collective-permute-start.55) | collective-permute-done | bytes 262176 | tf_op jit(solution)/shard_map/ppermute | solution.py:235
  431.3 13.7 %collective-permute-done.42.b_ref = bf16[64,1024]{1,0:T(8,128)(2,1)S(1)} collective-permute-done((bf16[64,1024]{1,0:T(8,128)(2,1)S(1)}, bf16[64,1024]{1,0:T(8,128)(2,1)S(1)}, u32[]{:S(2)}, u32[]{:S(2)}) %collective-permute-start.42) | collective-permute-done | bytes 131104 | tf_op jit(solution)/shard_map/ppermute | solution.py:235
  (504 shorter events, 232.1 us)
Async XLA Ops:
  64.0 35.5 %collective-permute-start.8 = (bf16[256,1024]{1,0:T(8,128)(2,1)S(1)}, bf16[256,1024]{1,0:T(8,128)(2,1)S(1)}, u32[]{:S(2)}, u32[]{:S(2)}) collective-permute-start(bf16[256,1024]{1,0:T(8,128)(2,1)S(1)} %get-tuple-element.181.c0.refs_7_), channel_id=1, source_target_pairs={{0,1},{1,0},{2,3},{3,2},{4,5},{5,4},{6,7},{7,6},{8,9},{9,8},{10,11... | collective-permute-start | bytes 1572872 | tf_op jit(solution)/shard_map/ppermute | solution.py:235
  65.8 33.3 %collective-permute-start.17 = (bf16[256,1024]{1,0:T(8,128)(2,1)S(1)}, bf16[256,1024]{1,0:T(8,128)(2,1)S(1)}, u32[]{:S(2)}, u32[]{:S(2)}) collective-permute-start(bf16[256,1024]{1,0:T(8,128)(2,1)S(1)} %shard_map.228), channel_id=1, source_target_pairs={{0,2},{1,3},{2,0},{3,1},{4,6},{5,7},{6,4},{7,5},{8,10},{9,11},{10,... | collective-permute-start | bytes 1572872 | tf_op jit(solution)/shard_map/ppermute | solution.py:235
  77.0 33.3 %collective-permute-start.6 = (bf16[256,1024]{1,0:T(8,128)(2,1)S(1)}, bf16[256,1024]{1,0:T(8,128)(2,1)S(1)}, u32[]{:S(2)}, u32[]{:S(2)}) collective-permute-start(bf16[256,1024]{1,0:T(8,128)(2,1)S(1)} %get-tuple-element.99.n0.refs_5_), channel_id=1, source_target_pairs={{0,2},{1,3},{2,0},{3,1},{4,6},{5,7},{6,4},{7,5},{8,10},{9,11},{10,... | collective-permute-start | bytes 1572872 | tf_op jit(solution)/shard_map/ppermute | solution.py:235
  79.1 42.4 %collective-permute-start.22 = (bf16[256,1024]{1,0:T(8,128)(2,1)S(1)}, bf16[256,1024]{1,0:T(8,128)(2,1)S(1)}, u32[]{:S(2)}, u32[]{:S(2)}) collective-permute-start(bf16[256,1024]{1,0:T(8,128)(2,1)S(1)} %get-tuple-element.180.c0.refs_3_), channel_id=1, source_target_pairs={{0,2},{1,3},{2,0},{3,1},{4,6},{5,7},{6,4},{7,5},{8,10},{9,11},{10,... | collective-permute-start | bytes 1572872 | tf_op jit(solution)/shard_map/ppermute | solution.py:235
  87.8 33.7 %collective-permute-start.10 = (bf16[256,1024]{1,0:T(8,128)(2,1)S(1)}, bf16[256,1024]{1,0:T(8,128)(2,1)S(1)}, u32[]{:S(2)}, u32[]{:S(2)}) collective-permute-start(bf16[256,1024]{1,0:T(8,128)(2,1)S(1)} %collective-permute-done.9.c2.refs_9_), channel_id=1, source_target_pairs={{0,1},{1,0},{2,3},{3,2},{4,5},{5,4},{6,7},{7,6},{8,9},{9,8},{10,11... | collective-permute-start | bytes 1572872 | tf_op jit(solution)/shard_map/ppermute | solution.py:235
  99.5 33.0 %collective-permute-start.19 = (bf16[256,1024]{1,0:T(8,128)(2,1)S(1)}, bf16[256,1024]{1,0:T(8,128)(2,1)S(1)}, u32[]{:S(2)}, u32[]{:S(2)}) collective-permute-start(bf16[256,1024]{1,0:T(8,128)(2,1)S(1)} %get-tuple-element.105.n0.refs_1_), channel_id=1, source_target_pairs={{0,2},{1,3},{2,0},{3,1},{4,6},{5,7},{6,4},{7,5},{8,10},{9,11},{10,... | collective-permute-start | bytes 1572872 | tf_op jit(solution)/shard_map/ppermute | solution.py:235
  150.1 33.5 %collective-permute-start.26 = (bf16[2,256,1024]{2,1,0:T(8,128)(2,1)}, bf16[2,256,1024]{2,1,0:T(8,128)(2,1)S(1)}, u32[]{:S(2)}, u32[]{:S(2)}) collective-permute-start(bf16[2,256,1024]{2,1,0:T(8,128)(2,1)} %get-tuple-element.109), channel_id=1, source_target_pairs={{0,1},{1,0},{2,3},{3,2},{4,5},{5,4},{6,7},{7,6},{8,9},{9,8},{10,11... | collective-permute-start | bytes 3145736 | tf_op jit(solution)/shard_map/ppermute | solution.py:235
  167.3 34.8 %collective-permute-start.33 = (bf16[2,256,1024]{2,1,0:T(8,128)(2,1)}, bf16[2,256,1024]{2,1,0:T(8,128)(2,1)S(1)}, u32[]{:S(2)}, u32[]{:S(2)}) collective-permute-start(bf16[2,256,1024]{2,1,0:T(8,128)(2,1)} %get-tuple-element.122), channel_id=1, source_target_pairs={{0,1},{1,0},{2,3},{3,2},{4,5},{5,4},{6,7},{7,6},{8,9},{9,8},{10,11... | collective-permute-start | bytes 3145736 | tf_op jit(solution)/shard_map/ppermute | solution.py:235
  182.0 46.4 %collective-permute-start.66 = (bf16[512,1024]{1,0:T(8,128)(2,1)}, bf16[512,1024]{1,0:T(8,128)(2,1)S(1)}, u32[]{:S(2)}, u32[]{:S(2)}) collective-permute-start(bf16[512,1024]{1,0:T(8,128)(2,1)} %get-tuple-element.167), channel_id=1, source_target_pairs={{0,4},{4,0},{8,12},{12,8},{16,20},{20,16},{24,28},{28,24},{1,5},{5... | collective-permute-start | bytes 3145736 | tf_op jit(solution)/shard_map/ppermute | solution.py:235
  228.4 54.8 %collective-permute-start.11 = (bf16[2,256,1024]{2,1,0:T(8,128)(2,1)S(1)}, bf16[2,256,1024]{2,1,0:T(8,128)(2,1)S(1)}, u32[]{:S(2)}, u32[]{:S(2)}) collective-permute-start(bf16[2,256,1024]{2,1,0:T(8,128)(2,1)S(1)} %copy-done.63), channel_id=1, source_target_pairs={{0,1},{1,0},{2,3},{3,2},{4,5},{5,4},{6,7},{7,6},{8,9},{9,8},{10,11... | collective-permute-start | bytes 3145736 | tf_op jit(solution)/shard_map/ppermute | solution.py:235
  230.3 53.7 %collective-permute-start.67 = (bf16[128,1024]{1,0:T(8,128)(2,1)}, bf16[128,1024]{1,0:T(8,128)(2,1)S(1)}, u32[]{:S(2)}, u32[]{:S(2)}) collective-permute-start(bf16[128,1024]{1,0:T(8,128)(2,1)} %get-tuple-element.169), channel_id=1, source_target_pairs={{0,8},{4,12},{8,0},{12,4},{16,24},{20,28},{24,16},{28,20},{1,9},{5... | collective-permute-start | bytes 786440 | tf_op jit(solution)/shard_map/ppermute | solution.py:235
  233.6 54.1 %collective-permute-start.68 = (bf16[128,1024]{1,0:T(8,128)(2,1)S(1)}, bf16[128,1024]{1,0:T(8,128)(2,1)S(1)}, u32[]{:S(2)}, u32[]{:S(2)}) collective-permute-start(bf16[128,1024]{1,0:T(8,128)(2,1)S(1)} %get-tuple-element.170), channel_id=1, source_target_pairs={{0,16},{4,20},{8,24},{12,28},{16,0},{20,4},{24,8},{28,12},{1,17},{... | collective-permute-start | bytes 786440 | tf_op jit(solution)/shard_map/ppermute | solution.py:235
  261.8 41.3 %collective-permute-start.75 = (bf16[128,1024]{1,0:T(8,128)(2,1)S(1)}, bf16[128,1024]{1,0:T(8,128)(2,1)S(1)}, u32[]{:S(2)}, u32[]{:S(2)}) collective-permute-start(bf16[128,1024]{1,0:T(8,128)(2,1)S(1)} %get-tuple-element.177), channel_id=1, source_target_pairs={{0,8},{4,12},{8,0},{12,4},{16,24},{20,28},{24,16},{28,20},{1,9},{5... | collective-permute-start | bytes 786440 | tf_op jit(solution)/shard_map/ppermute | solution.py:235
  287.7 44.4 %collective-permute-start.31 = (bf16[2,256,1024]{2,1,0:T(8,128)(2,1)}, bf16[2,256,1024]{2,1,0:T(8,128)(2,1)S(1)}, u32[]{:S(2)}, u32[]{:S(2)}) collective-permute-start(bf16[2,256,1024]{2,1,0:T(8,128)(2,1)} %get-tuple-element.119), channel_id=1, source_target_pairs={{0,1},{1,0},{2,3},{3,2},{4,5},{5,4},{6,7},{7,6},{8,9},{9,8},{10,11... | collective-permute-start | bytes 3145736 | tf_op jit(solution)/shard_map/ppermute | solution.py:235
  287.7 40.4 %collective-permute-start.38 = (bf16[2,256,1024]{2,1,0:T(8,128)(2,1)}, bf16[2,256,1024]{2,1,0:T(8,128)(2,1)S(1)}, u32[]{:S(2)}, u32[]{:S(2)}) collective-permute-start(bf16[2,256,1024]{2,1,0:T(8,128)(2,1)} %get-tuple-element.132), channel_id=1, source_target_pairs={{0,1},{1,0},{2,3},{3,2},{4,5},{5,4},{6,7},{7,6},{8,9},{9,8},{10,11... | collective-permute-start | bytes 3145736 | tf_op jit(solution)/shard_map/ppermute | solution.py:235
  303.1 60.5 %collective-permute-start.50 = (bf16[512,1024]{1,0:T(8,128)(2,1)}, bf16[512,1024]{1,0:T(8,128)(2,1)}, u32[]{:S(2)}, u32[]{:S(2)}) collective-permute-start(bf16[512,1024]{1,0:T(8,128)(2,1)} %get-tuple-element.151), channel_id=1, source_target_pairs={{0,4},{4,0},{8,12},{12,8},{16,20},{20,16},{24,28},{28,24},{1,5},{5... | collective-permute-start | bytes 3145736 | tf_op jit(solution)/shard_map/ppermute | solution.py:235
  332.1 34.1 %collective-permute-start.39 = (bf16[256,1024]{1,0:T(8,128)(2,1)}, bf16[256,1024]{1,0:T(8,128)(2,1)}, u32[]{:S(2)}, u32[]{:S(2)}) collective-permute-start(bf16[256,1024]{1,0:T(8,128)(2,1)} %shard_map.241), channel_id=1, source_target_pairs={{0,2},{1,3},{2,0},{3,1},{4,6},{5,7},{6,4},{7,5},{8,10},{9,11},{10,... | collective-permute-start | bytes 1572872 | tf_op jit(solution)/shard_map/ppermute | solution.py:235
  335.2 33.9 %collective-permute-start.32 = (bf16[256,1024]{1,0:T(8,128)(2,1)}, bf16[256,1024]{1,0:T(8,128)(2,1)}, u32[]{:S(2)}, u32[]{:S(2)}) collective-permute-start(bf16[256,1024]{1,0:T(8,128)(2,1)} %shard_map.237), channel_id=1, source_target_pairs={{0,2},{1,3},{2,0},{3,1},{4,6},{5,7},{6,4},{7,5},{8,10},{9,11},{10,... | collective-permute-start | bytes 1572872 | tf_op jit(solution)/shard_map/ppermute | solution.py:235
  351.3 45.0 %collective-permute-start.24 = (bf16[2,256,1024]{2,1,0:T(8,128)(2,1)}, bf16[2,256,1024]{2,1,0:T(8,128)(2,1)}, u32[]{:S(2)}, u32[]{:S(2)}) collective-permute-start(bf16[2,256,1024]{2,1,0:T(8,128)(2,1)} %get-tuple-element.107), channel_id=1, source_target_pairs={{0,1},{1,0},{2,3},{3,2},{4,5},{5,4},{6,7},{7,6},{8,9},{9,8},{10,11... | collective-permute-start | bytes 3145736 | tf_op jit(solution)/shard_map/ppermute | solution.py:235
  363.6 34.2 %collective-permute-start.12 = (bf16[256,1024]{1,0:T(8,128)(2,1)}, bf16[256,1024]{1,0:T(8,128)(2,1)}, u32[]{:S(2)}, u32[]{:S(2)}) collective-permute-start(bf16[256,1024]{1,0:T(8,128)(2,1)} %shard_map.225), channel_id=1, source_target_pairs={{0,2},{1,3},{2,0},{3,1},{4,6},{5,7},{6,4},{7,5},{8,10},{9,11},{10,... | collective-permute-start | bytes 1572872 | tf_op jit(solution)/shard_map/ppermute | solution.py:235
  393.6 98.9 %collective-permute-start.73 = (bf16[512,1024]{1,0:T(8,128)(2,1)S(1)}, bf16[512,1024]{1,0:T(8,128)(2,1)S(1)}, u32[]{:S(2)}, u32[]{:S(2)}) collective-permute-start(bf16[512,1024]{1,0:T(8,128)(2,1)S(1)} %shard_map.261.a_ref), channel_id=1, source_target_pairs={{0,4},{4,0},{8,12},{12,8},{16,20},{20,16},{24,28},{28,24},{1,5},{5... | collective-permute-start | bytes 3145736 | tf_op jit(solution)/shard_map/ppermute | solution.py:235
  396.2 99.1 %collective-permute-start.81 = (bf16[512,1024]{1,0:T(8,128)(2,1)S(1)}, bf16[512,1024]{1,0:T(8,128)(2,1)S(1)}, u32[]{:S(2)}, u32[]{:S(2)}) collective-permute-start(bf16[512,1024]{1,0:T(8,128)(2,1)S(1)} %shard_map.266.a_ref), channel_id=1, source_target_pairs={{0,4},{4,0},{8,12},{12,8},{16,20},{20,16},{24,28},{28,24},{1,5},{5... | collective-permute-start | bytes 3145736 | tf_op jit(solution)/shard_map/ppermute | solution.py:235
  427.6 59.8 %collective-permute-start.25 = (bf16[256,1024]{1,0:T(8,128)(2,1)S(1)}, bf16[256,1024]{1,0:T(8,128)(2,1)S(1)}, u32[]{:S(2)}, u32[]{:S(2)}) collective-permute-start(bf16[256,1024]{1,0:T(8,128)(2,1)S(1)} %shard_map.231), channel_id=1, source_target_pairs={{0,2},{1,3},{2,0},{3,1},{4,6},{5,7},{6,4},{7,5},{8,10},{9,11},{10,... | collective-permute-start | bytes 1572872 | tf_op jit(solution)/shard_map/ppermute | solution.py:235
  430.8 72.8 %collective-permute-start.57 = (bf16[512,1024]{1,0:T(8,128)(2,1)}, bf16[512,1024]{1,0:T(8,128)(2,1)}, u32[]{:S(2)}, u32[]{:S(2)}) collective-permute-start(bf16[512,1024]{1,0:T(8,128)(2,1)} %shard_map.251.a_ref), channel_id=1, source_target_pairs={{0,4},{4,0},{8,12},{12,8},{16,20},{20,16},{24,28},{28,24},{1,5},{5... | collective-permute-start | bytes 3145736 | tf_op jit(solution)/shard_map/ppermute | solution.py:235
  (205 other events, 2985.5 us)

commit v2 on v0

v2 whole, which is shorter than its diff:
```python
import functools
import math

import jax
import jax.numpy as jnp
from jax import lax
from jax.experimental import pallas as pl
from jax.experimental.pallas import tpu as pltpu
from jax.sharding import PartitionSpec as P

HD = 128
BLK = 512
CTX = 128
HEAD = BLK - CTX
NS = 16
EPS = 1e-05
SCALE = 1.0 / math.sqrt(HD)
SCALE2 = SCALE * math.log2(math.e)
NEG = -1e30
F32 = jnp.float32
BF16 = jnp.bfloat16

VMEM = pl.BlockSpec(memory_space=pltpu.VMEM)
SMEM = pl.BlockSpec(memory_space=pltpu.SMEM)
ANY = pl.BlockSpec(memory_space=pl.ANY)


def params(mib):
    return pltpu.CompilerParams(vmem_limit_bytes=mib << 20)


def cost(flops, nbytes):
    return pl.CostEstimate(flops=int(flops), bytes_accessed=int(nbytes), transcendentals=0)


def dot(a, b):
    return lax.dot_general(a, b, (((1,), (0,)), ((), ())), preferred_element_type=F32)


def dot_nt(a, b):
    return lax.dot_general(a, b, (((1,), (1,)), ((), ())), preferred_element_type=F32)


def dot_tn(a, b):
    return lax.dot_general(a, b, (((0,), (0,)), ((), ())), preferred_element_type=F32)


def shape(dims, kind):
    return jax.ShapeDtypeStruct(dims, kind)


def triangle(upper):
    row = lax.broadcasted_iota(jnp.int32, (CTX, 2 * CTX), 0)
    col = lax.broadcasted_iota(jnp.int32, (CTX, 2 * CTX), 1) % CTX
    keep = (row <= col) if upper else (row >= col)
    return jnp.where(keep, 1.0, 0.0).astype(BF16)


def running(tri, values):
    high = values.astype(BF16)
    rest = (values - high.astype(F32)).astype(BF16)
    return dot(tri, jnp.concatenate([high, rest], axis=0))


def head_sums(u_ref, rate_ref, moment):
    width = rate_ref.shape[1]
    place = lax.broadcasted_iota(jnp.int32, (8, width), 0).astype(F32)
    sums, moments = [], []
    group = 4 if moment else 8
    for base in range(0, NS, group):
        rates = [rate_ref[n : n + 1, :] for n in range(base, base + group)]
        steps = [jnp.broadcast_to(jnp.exp(-8.0 * r), (8, width)) for r in rates]

        def body(chunk, carry):
            start = pl.multiple_of(chunk * 8, 8)
            rows = u_ref[pl.ds(start, 8), :]
            first = [acc * step + rows for acc, step in zip(carry[0], steps)]
            if not moment:
                return (first, carry[1])
            scaled = rows * (place + (chunk * 8 - HEAD).astype(F32))
            second = [acc * step + scaled for acc, step in zip(carry[1], steps)]
            return (first, second)

        zero = [jnp.zeros((8, width), F32) for _ in range(group)]
        first, second = lax.fori_loop(
            0, HEAD // 8, body, (zero, list(zero) if moment else []), unroll=4
        )
        for k, rate in enumerate(rates):
            last = jnp.exp(rate * (place - 8.0))
            sums.append(jnp.sum(first[k] * last, axis=0, keepdims=True))
            if moment:
                moments.append(jnp.sum(second[k] * last, axis=0, keepdims=True))
    return sums, moments


def state_forward(u_ref, rate_ref, in_ref, out_ref):
    width = rate_ref.shape[1]
    sums, _ = head_sums(u_ref, rate_ref, False)
    tail = u_ref[pl.ds(HEAD, CTX), :]
    time = lax.broadcasted_iota(jnp.int32, (CTX, width), 0).astype(F32)
    tri = triangle(False)
    total = jnp.zeros((CTX, width), F32)
    for n in range(NS):
        rate = rate_ref[n : n + 1, :]
        gain = in_ref[n : n + 1, :] * jnp.sqrt(1.0 - jnp.exp(-2.0 * rate))
        weight = gain * out_ref[n : n + 1, :]
        prefix = running(tri, jnp.exp(rate * time) * tail)
        total = total + weight * (jnp.exp(-rate * time) * (sums[n] + prefix))
    return total


def state_backward(grad, u_ref, du_ref, rate_ref, in_ref, out_ref, gs_ref):
    width = rate_ref.shape[1]
    sums, moments = head_sums(u_ref, rate_ref, True)
    tail = u_ref[pl.ds(HEAD, CTX), :]
    time = lax.broadcasted_iota(jnp.int32, (CTX, width), 0).astype(F32)
    place = lax.broadcasted_iota(jnp.int32, (8, width), 0).astype(F32)
    lower, upper = triangle(False), triangle(True)
    total = jnp.zeros((CTX, width), F32)
    starts = []
    for n in range(NS):
        rate = rate_ref[n : n + 1, :]
        root = jnp.sqrt(1.0 - jnp.exp(-2.0 * rate))
        enter = in_ref[n : n + 1, :]
        leave = out_ref[n : n + 1, :]
        gain = enter * root
        rising = jnp.exp(rate * time)
        driven = rising * tail
        states = sums[n] + running(lower, driven)
        seen = jnp.exp(-rate * time) * grad
        later = running(upper, seen)
        product = seen * states
        energy = jnp.sum(product, axis=0, keepdims=True)
        slope = jnp.sum(time * (product - driven * later), axis=0, keepdims=True)
        slope = slope - later[0:1] * moments[n]
        total = total + (gain * leave) * (rising * later)
        starts.append((gain * leave) * later[0:1])
        gs_ref[0, n : n + 1, :] = leave * (
            energy * enter * jnp.exp(-2.0 * rate) / root - gain * slope
        )
        gs_ref[1, n : n + 1, :] = leave * energy * root
        gs_ref[2, n : n + 1, :] = gain * energy
    du_ref[pl.ds(HEAD, CTX), :] = total
    group = 8
    for base in range(0, NS, group):
        rates = [rate_ref[n : n + 1, :] for n in range(base, base + group)]
        steps = [jnp.broadcast_to(jnp.exp(-8.0 * r), (8, width)) for r in rates]
        begin = [
            starts[base + k] * jnp.exp(rate * (place - 8.0)) for k, rate in enumerate(rates)
        ]

        def body(index, carry):
            start = pl.multiple_of(HEAD - 8 - index * 8, 8)
            value = functools.reduce(lambda a, b: a + b, carry)
            if base:
                value = value + du_ref[pl.ds(start, 8), :]
            du_ref[pl.ds(start, 8), :] = value
            return [c * step for c, step in zip(carry, steps)]

        lax.fori_loop(0, HEAD // 8, body, begin, unroll=4)


def layout_scalars(len_ref, micro):
    first, second = len_ref[micro, 0], len_ref[micro, 1]
    first_blocks = (first + (BLK - 1)) // BLK
    second_blocks = (second + (BLK - 1)) // BLK
    docs, valid = [], []
    for b in range(2):
        doc = jnp.where(b < first_blocks, 0, jnp.where(b < first_blocks + second_blocks, 1, 2))
        start = jnp.where(doc == 0, 0, first_blocks)
        extent = jnp.where(doc == 0, first, jnp.where(doc == 1, second, 0))
        docs.append(doc)
        valid.append(extent - (b - start) * BLK)
    return valid, docs[0] == docs[1]


class Copies:
    def __init__(self, send, recv):
        self.send, self.recv, self.used, self.open = send, recv, 0, []

    def start(self, source, target, device):
        copy = pltpu.make_async_remote_copy(
            src_ref=source,
            dst_ref=target,
            send_sem=self.send.at[self.used],
            recv_sem=self.recv.at[self.used],
            device_id=device,
            device_id_type=pl.DeviceIdType.MESH,
        )
        self.used += 1
        copy.start()
        self.open.append(copy)
        return copy

    def sent(self, copy):
        copy.wait_send()
        self.open = [other for other in self.open if other is not copy]

    def drain(self):
        for copy in self.open:
            copy.wait_send()
        self.open = []


class Moves:
    def __init__(self, sems):
        self.sems, self.used = sems, 0

    def start(self, source, target):
        copy = pltpu.make_async_copy(source, target, self.sems.at[self.used])
        self.used += 1
        copy.start()
        return copy


def layer(
    nz, tokens, lengths, cotangent, gain_one, gain_two, w_in, ssm, ctx_w, w_out, w_up, w_down
):
    count, rows, width = tokens.shape
    chans = w_out.shape[0]
    heads = chans // HD
    hidden = w_up.shape[1]
    total = 4 * rows
    pair = 2 * rows
    small_rows = heads * CTX + 3 * NS + 8
    unit = 2 * nz * 16
    misc_rows = width + small_rows + (-small_rows % unit)
    sizes = dict(down=(hidden, width), up=(width, hidden), inp=(width, 4 * chans), misc=(misc_rows, chans))
    names = list(sizes)
    root = math.sqrt(2.0 / math.pi)
    n_remote = 51 + 4 * (1 + 2 * (nz - 1) + nz)
    n_local = 24 + 4 * nz

    def kernel(*refs):
        (
            len_ref, tok, cot_hbm, g1, g2, in_hbm, rate, enter, leave, cw, out_hbm, up_hbm, down_hbm,
        ) = refs[:13]
        mixed_hbm, gtok_hbm, pr_hbm = refs[13:16]
        grads = dict(zip(names, refs[16:20]))
        ry = dict(zip(names, refs[20:24]))
        rz = dict(zip(names, refs[24:28]))
        (
            w_i, w_o, w_u, w_d, xn, cot, n2, gbr, hid, gbf, qkv, u0, pr, ho, cx, ckv, dh, gctx,
            give, keep_a, keep_b, sib_a, sib_b, far_a, far_b, mid, acc, tmp, misc,
            gain_acc, gain_got, gcw, gss, send_sems, recv_sems, local_sems,
        ) = refs[28:]
        me = lax.axis_index("mp")
        core, chip = me % 2, me // 2
        near, far, both = chip * 2 + 1 - core, (1 - chip) * 2 + core, (1 - chip) * 2 + 1 - core
        dp = lax.axis_index("dp")
        y, z = dp % 2, dp // 2
        to_near, to_far, to_both = {"mp": near}, {"mp": far}, {"mp": both}
        to_y = {"dp": z * 2 + 1 - y}
        zs = [(z + k) % nz for k in range(nz)]
        to_z = [{"dp": zk * 2 + y} for zk in zs]
        remote, local = Copies(send_sems, recv_sems), Moves(local_sems)

        loads = {
            "in": local.start(in_hbm, w_i),
            "cot0": local.start(cot_hbm.at[0], cot.at[0, me]),
            "cot1": local.start(cot_hbm.at[1], cot.at[1, me]),
            "out": local.start(out_hbm, w_o),
            "up": local.start(up_hbm, w_u),
            "down": local.start(down_hbm, w_d),
        }
        barrier = pltpu.get_barrier_semaphore()
        for device in [to_near, to_far, to_both, to_y] + to_z[1:]:
            pl.semaphore_signal(
                barrier, inc=1, device_id=device, device_id_type=pl.DeviceIdType.MESH
            )
        pl.semaphore_wait(barrier, 3 + nz)

        def share(buf, m):
            return remote.start(buf.at[m, me], buf.at[m, me], to_near)

        def cross(buf, m):
            return remote.start(buf.at[m, me], buf.at[m, me], to_far)

        def pass_on(buf, m, copy):
            copy.wait_recv()
            return remote.start(buf.at[m, far], buf.at[m, far], to_near)

        def offer(kind, slot, sib, m):
            return remote.start(give.at[kind, slot], sib.at[m, slot], to_near)

        def by_rows(work):
            step = 64

            def body(i, carry):
                work(pl.ds(pl.multiple_of(i * step, step), step))
                return carry

            lax.fori_loop(0, rows // step, body, 0)

        def owed(offers, keep, sib, far_buf, m):
            offers[1].wait_recv()

            def work(at):
                keep[m, 1, at, :] = (
                    keep[m, 1, at, :].astype(F32) + sib[m, 1, at, :].astype(F32)
                ).astype(BF16)

            by_rows(work)
            return remote.start(keep.at[m, 1], far_buf.at[m], to_far)

        def summed(offers, copy, keep, sib, far_buf, m):
            offers[0].wait_recv()
            copy.wait_recv()
            return lambda at: (
                keep[m, 0, at, :].astype(F32)
                + sib[m, 0, at, :].astype(F32)
                + far_buf[m, at, :].astype(F32)
            )

        def inverse_root(value):
            return lax.rsqrt(jnp.mean(value * value, axis=-1, keepdims=True) + EPS)

        def norm_first(m):
            def work(at):
                x = tok[m, at, :].astype(F32)
                xn[m, me, at, :] = (x * inverse_root(x) * g1[...]).astype(BF16)

            by_rows(work)

        def norm_second(m, branch):
            def work(at):
                value = tok[m, at, :].astype(F32) + branch(at)
                mid[m, at, :] = value
                n2[m, me, at, :] = (value * inverse_root(value) * g2[...]).astype(BF16)

            by_rows(work)

        def pulled(value, grad, gain, line):
            scale = inverse_root(value)
            unit_row = value * scale
            gain_acc[line : line + 1, :] += jnp.sum(grad * unit_row, axis=0, keepdims=True)
            inner = grad * gain[...]
            return scale * (inner - unit_row * jnp.mean(inner * unit_row, axis=-1, keepdims=True))

        def norm_second_back(m, grad):
            def work(at):
                value = cot[m, me, at, :].astype(F32) + pulled(mid[m, at, :], grad(at), g2, 1)
                gbr[m, me, at, :] = value.astype(BF16)

            by_rows(work)

        def norm_first_back(m, grad):
            def work(at):
                x = tok[m, at, :].astype(F32)
                mid[m, at, :] = gbr[m, me, at, :].astype(F32) + pulled(x, grad(at), g1, 0)

            by_rows(work)
            return local.start(mid.at[m], gtok_hbm.at[m])

        def mix(m, branch):
            def work(at):
                keep_a[m, 0, at, :] = (mid[m, at, :] + branch(at)).astype(BF16)

            by_rows(work)
            return local.start(keep_a.at[m, 0], mixed_hbm.at[m])

        def project(m, side):
            def body(i, carry):
                t = side * 2 + i
                at = pl.ds(pl.multiple_of(t * rows, rows), rows)
                x = xn[m, t]
                qkv[m, at, :] = dot(x, w_i[:, : 3 * chans]).astype(BF16)

                @pl.when(t < 2)
                def _():
                    u0[m, at, :] = dot(x, w_i[:, 3 * chans :])

                return carry

            lax.fori_loop(0, 2, body, 0)

        def scan(m):
            context = state_forward(u0.at[m], rate, enter, leave).astype(BF16)
            cx[m] = context
            for h in range(heads):
                ckv[m, h] = dot(context[:, h * HD : (h + 1) * HD], cw[h]).astype(BF16)

        def attend(m):
            valid, linked = layout_scalars(len_ref, m)
            for h in range(heads):
                lanes = slice(h * HD, (h + 1) * HD)
                klanes = slice(chans + h * HD, chans + (h + 1) * HD)
                vlanes = slice(2 * chans + h * HD, 2 * chans + (h + 1) * HD)
                for b in range(2):
                    for half in range(2):
                        row0 = half * rows
                        keys = row0 + rows
                        spot = b * BLK + row0
                        q = qkv[m, spot : spot + rows, lanes]
                        k = qkv[m, b * BLK : b * BLK + keys, klanes]
                        v = qkv[m, b * BLK : b * BLK + keys, vlanes]
                        s = dot_nt(q, k) * SCALE2
                        row = lax.broadcasted_iota(jnp.int32, (rows, keys), 0) + row0
                        col = lax.broadcasted_iota(jnp.int32, (rows, keys), 1)
                        allowed = (col < jnp.minimum(row, valid[b])) | (col == row)
                        s = jnp.where(allowed, s, NEG)
                        peak = jnp.max(s, axis=-1, keepdims=True)
                        if b:
                            sc = dot_nt(q, ckv[m, h, :, :HD]) * SCALE2
                            sc = jnp.where(linked, sc, NEG)
                            peak = jnp.maximum(peak, jnp.max(sc, axis=-1, keepdims=True))
                            ec = jnp.exp2(sc - peak)
                        e = jnp.exp2(s - peak)
                        norm = jnp.sum(e, axis=-1, keepdims=True)
                        if b:
                            norm = norm + jnp.sum(ec, axis=-1, keepdims=True)
                        inverse = 1.0 / norm
                        p = (e * inverse).astype(BF16)
                        pr[h, b, row0 : row0 + rows, CTX : CTX + keys] = p
                        o = dot(p, v)
                        if b:
                            pc = (ec * inverse).astype(BF16)
                            pr[h, b, row0 : row0 + rows, :CTX] = pc
                            o = o + dot(pc, ckv[m, h, :, HD:])
                        ho[m, 2 * b + half, :, lanes] = o.astype(BF16)

        def spread(product, keep, kind, sib, m, before):
            for copy in before:
                remote.sent(copy)
            give[kind, 1] = product(both).astype(BF16)
            second = offer(kind, 1, sib, m)
            give[kind, 0] = product(near).astype(BF16)
            first = offer(kind, 0, sib, m)
            keep[m, 1] = product(far).astype(BF16)
            keep[m, 0] = product(me).astype(BF16)
            return [first, second]

        def feed(m, side, other):
            slot = 1 if other else 0

            def body(i, carry):
                t = side * 2 + jnp.where(i == 0, 1 - core, core)
                for start in range(0, hidden, 256):
                    cut = slice(start, start + 256)
                    before = dot(n2[m, t], w_u[:, cut])
                    square = before * before
                    th = jnp.tanh(root * (before * (1.0 + 0.044715 * square)))
                    half = 0.5 + 0.5 * th
                    hid[m, t, :, cut] = (before * half).astype(BF16)
                    slope = half + (0.5 * root) * before * (1.0 - th * th) * (
                        1.0 + 0.134145 * square
                    )
                    gbf[m, t, :, cut] = (dot_nt(cot[m, t], w_d[cut, :]) * slope).astype(BF16)
                branch = dot(hid[m, t], w_d[...]).astype(BF16)
                gn = dot_nt(gbf[m, t], w_u[...]).astype(BF16)

                @pl.when(i == 0)
                def _():
                    give[0, slot] = branch
                    give[1, slot] = gn

                @pl.when(i == 1)
                def _():
                    keep_a[m, slot] = branch
                    keep_b[m, slot] = gn

                return carry

            lax.fori_loop(0, 2, body, 0)
            return offer(0, slot, sib_a, m), offer(1, slot, sib_b, m)

        def heads_back(m, side):
            def body(i, carry):
                t = side * 2 + i
                at = pl.ds(pl.multiple_of(t * rows, rows), rows)
                dh[at, :] = dot_nt(gbr[m, t], w_o[...]).astype(BF16)
                return carry

            lax.fori_loop(0, 2, body, 0)

        def attend_back(m):
            for h in range(heads):
                lanes = slice(h * HD, (h + 1) * HD)
                klanes = slice(chans + h * HD, chans + (h + 1) * HD)
                vlanes = slice(2 * chans + h * HD, 2 * chans + (h + 1) * HD)
                for b in range(2):
                    grad_k, grad_v = [None, None], [None, None]
                    grad_c = grad_cv = None
                    for half in (1, 0):
                        row0 = half * rows
                        keys = row0 + rows
                        spot = slice(b * BLK + row0, b * BLK + row0 + rows)
                        go = dh[spot, lanes]
                        qh = qkv[m, spot, lanes]
                        kh = qkv[m, b * BLK : b * BLK + keys, klanes]
                        vh = qkv[m, b * BLK : b * BLK + keys, vlanes]
                        p = pr[h, b, row0 : row0 + rows, CTX : CTX + keys]
                        pf = p.astype(F32)
                        dprob = dot_nt(go, vh)
                        delta = jnp.sum(dprob * pf, axis=-1, keepdims=True)
                        if b:
                            pc = pr[h, b, row0 : row0 + rows, :CTX]
                            pcf = pc.astype(F32)
                            dpc = dot_nt(go, ckv[m, h, :, HD:])
                            delta = delta + jnp.sum(dpc * pcf, axis=-1, keepdims=True)
                            dsc = (pcf * (dpc - delta)).astype(BF16)
                        ds = (pf * (dprob - delta)).astype(BF16)
                        dq = dot(ds, kh)
                        if b:
                            dq = dq + dot(dsc, ckv[m, h, :, :HD])
                            one = dot_tn(dsc, qh)
                            two = dot_tn(pc, go)
                            grad_c = one if grad_c is None else grad_c + one
                            grad_cv = two if grad_cv is None else grad_cv + two
                        hid[m, 2 * b + half, :, lanes] = (dq * SCALE).astype(BF16)
                        dk = dot_tn(ds, qh)
                        dv = dot_tn(p, go)
                        if half:
                            grad_k = [dk[:rows], dk[rows:]]
                            grad_v = [dv[:rows], dv[rows:]]
                        else:
                            grad_k[0] = grad_k[0] + dk
                            grad_v[0] = grad_v[0] + dv
                    for part in range(2):
                        t = 2 * b + part
                        hid[m, t, :, klanes] = (grad_k[part] * SCALE).astype(BF16)
                        hid[m, t, :, vlanes] = grad_v[part].astype(BF16)
                    if b:
                        low_c = (grad_c * SCALE).astype(BF16)
                        low_cv = grad_cv.astype(BF16)
                        ch = cx[m, :, lanes]
                        gcw[m, h, :, :HD] = dot_tn(ch, low_c)
                        gcw[m, h, :, HD:] = dot_tn(ch, low_cv)
                        gctx[:, lanes] = dot_nt(low_c, cw[h, :, :HD]) + dot_nt(
                            low_cv, cw[h, :, HD:]
                        )

        def scan_back(m):
            state_backward(gctx[...], u0.at[m], u0.at[m], rate, enter, leave, gss.at[m])
            for t in range(2):
                hid[m, t, :, 3 * chans :] = u0[m, t * rows : (t + 1) * rows, :].astype(BF16)
                hid[m, 2 + t, :, 3 * chans :] = jnp.zeros((rows, chans), BF16)

        def gather_tile(left, right, tile):
            lanes = pl.ds(pl.multiple_of(tile * rows, rows), rows)
            acc[...] = jnp.zeros_like(acc)

            def body(i, carry):
                m, t = i // 4, i % 4
                acc[...] += dot_tn(left[m, t, :, lanes], right[m, t])
                return carry

            lax.fori_loop(0, 4 * count, body, 0)

        def tiles(left, right, stage, which):
            span = stage.shape[0] // (2 * rows)

            def body(i, carry):
                tile = which * span + i
                gather_tile(left, right, tile)
                at = pl.ds(pl.multiple_of(tile * rows, rows), rows)
                stage[at, :] = acc[...].astype(BF16)
                return carry

            lax.fori_loop(0, span, body, 0)

        def part(ref, start, size):
            return ref.at[pl.ds(pl.multiple_of(start, 16), size), :]

        def swap_y(name, stage):
            span = sizes[name][0] // 2
            return remote.start(part(stage, (1 - y) * span, span), ry[name], to_y)

        def landing(name, row, size):
            if sizes[name][1] != width:
                return tmp.at[pl.ds(row, size), :]
            return gbf.at[0, row // rows, pl.ds(row % rows, size), :]

        def sum_y(name, stage, copy):
            span = sizes[name][0] // 2
            piece, block = span // nz, min(span, rows) if sizes[name][1] == width else span
            copy.wait_recv()
            spots = range(0, span, block)
            moves = [
                local.start(ry[name].at[pl.ds(row, block), :], landing(name, row, block))
                for row in spots
            ]
            for row, move in zip(spots, moves):
                move.wait()
                at = pl.ds(pl.multiple_of(y * span + row, 16), block)
                got = landing(name, row, block)
                stage[at, :] = (stage[at, :].astype(F32) + got[...].astype(F32)).astype(BF16)
            return [
                remote.start(part(stage, y * span + zs[k] * piece, piece), rz[name].at[k - 1], to_z[k])
                for k in range(1, nz)
            ]

        def sum_z(name, stage, copies):
            span = sizes[name][0] // 2
            piece = span // nz
            for copy in copies:
                copy.wait_recv()
            moves = [
                local.start(rz[name].at[k], landing(name, k * piece, piece)) for k in range(nz - 1)
            ]
            for move in moves:
                move.wait()
            spot = y * span + z * piece
            at = pl.ds(pl.multiple_of(spot, 16), piece)
            value = stage[at, :].astype(F32)
            for k in range(nz - 1):
                value = value + landing(name, k * piece, piece)[...].astype(F32)
            stage[at, :] = value.astype(BF16)
            mine = part(stage, spot, piece)
            place = part(grads[name], spot, piece)
            outs = [remote.start(mine, place, to_z[k]) for k in range(1, nz)]
            last = [remote.start(mine, place, to_y)]
            return outs, last, local.start(mine, place)

        def spread_y(name, state):
            high, _ = sizes[name]
            span, piece = high // 2, high // 2 // nz
            outs, last, move = state
            for k in range(1, nz):
                outs[k - 1].wait_recv()
                place = part(grads[name], y * span + ((z + nz - k) % nz) * piece, piece)
                last.append(remote.start(place, place, to_y))
            return last, move

        def finish(state):
            last, move = state
            for copy in last:
                copy.wait_recv()
            move.wait()

        gain_acc[...] = jnp.zeros_like(gain_acc)
        norm_first(0)
        n_near = [share(xn, 0), None]
        n_far = [cross(xn, 0), None]
        norm_first(1)
        n_near[1] = share(xn, 1)
        loads["cot0"].wait()
        loads["cot1"].wait()
        c_near = [share(cot, 0), share(cot, 1)]
        loads["in"].wait()
        n_near[0].wait_recv()
        project(0, chip)
        n_both = [pass_on(xn, 0, n_far[0]), None]
        n_far[1] = cross(xn, 1)
        n_both[0].wait_recv()
        project(0, 1 - chip)
        scan(0)
        attend(0)
        save = local.start(pr, pr_hbm.at[0])
        n_both[1] = pass_on(xn, 1, n_far[1])
        c_far = [cross(cot, 0), None]
        loads["out"].wait()
        offers = [spread(lambda t: dot(ho[0, t], w_o[...]), keep_a, 0, sib_a, 0, []), None]
        n_near[1].wait_recv()
        project(1, chip)
        branch_far = [owed(offers[0], keep_a, sib_a, far_a, 0), None]
        n_both[1].wait_recv()
        project(1, 1 - chip)
        scan(1)
        save.wait()
        attend(1)
        save = local.start(pr, pr_hbm.at[1])
        c_both = [pass_on(cot, 0, c_far[0]), None]
        offers[1] = spread(
            lambda t: dot(ho[1, t], w_o[...]), keep_a, 0, sib_a, 1, offers[0]
        )
        branch_far[1] = owed(offers[1], keep_a, sib_a, far_a, 1)
        norm_second(0, summed(offers[0], branch_far[0], keep_a, sib_a, far_a, 0))
        m_near = [share(n2, 0), None]
        m_far = [cross(n2, 0), None]
        loads["up"].wait()
        loads["down"].wait()
        c_near[0].wait_recv()
        m_near[0].wait_recv()
        for copy in offers[1]:
            remote.sent(copy)
        remote.sent(branch_far[0])
        feed_offers = [[None, None], [None, None]]
        first = feed(0, chip, False)
        norm_second(1, summed(offers[1], branch_far[1], keep_a, sib_a, far_a, 1))
        m_near[1] = share(n2, 1)
        m_both = [pass_on(n2, 0, m_far[0]), None]
        m_far[1] = cross(n2, 1)
        c_far[1] = cross(cot, 1)
        c_both[0].wait_recv()
        m_both[0].wait_recv()
        second = feed(0, 1 - chip, True)
        out_offers = [(first[0], second[0]), None]
        back_offers = [(first[1], second[1]), None]
        back_far = [owed(back_offers[0], keep_b, sib_b, far_b, 0), None]
        c_near[1].wait_recv()
        m_near[1].wait_recv()
        remote.sent(branch_far[1])
        for copy in (first[0], first[1]):
            remote.sent(copy)
        first = feed(1, chip, False)
        m_both[1] = pass_on(n2, 1, m_far[1])
        c_both[1] = pass_on(cot, 1, c_far[1])
        m_both[1].wait_recv()
        c_both[1].wait_recv()
        for copy in (second[0], second[1]):
            remote.sent(copy)
        second = feed(1, 1 - chip, True)
        out_offers[1] = (first[0], second[0])
        back_offers[1] = (first[1], second[1])
        back_far[1] = owed(back_offers[1], keep_b, sib_b, far_b, 1)
        save.wait()
        fetch = local.start(pr_hbm.at[0], pr)
        norm_second_back(0, summed(back_offers[0], back_far[0], keep_b, sib_b, far_b, 0))
        b_near = [share(gbr, 0), None]
        b_far = [cross(gbr, 0), None]
        tiles(hid, cot, w_d, 1 - y)
        down = swap_y("down", w_d)
        out_far = [owed(out_offers[0], keep_a, sib_a, far_a, 0), None]
        norm_second_back(1, summed(back_offers[1], back_far[1], keep_b, sib_b, far_b, 1))
        b_near[1] = share(gbr, 1)
        b_both = [pass_on(gbr, 0, b_far[0]), None]
        b_far[1] = cross(gbr, 1)
        tiles(hid, cot, w_d, y)
        tiles(n2, gbf, w_u, 1 - y)
        up = swap_y("up", w_u)
        tiles(n2, gbf, w_u, y)
        for copy in (first[0], first[1], second[0], second[1], back_far[0]):
            remote.sent(copy)
        b_near[0].wait_recv()
        b_both[0].wait_recv()
        heads_back(0, 0)
        heads_back(0, 1)
        fetch.wait()
        attend_back(0)
        fetch = local.start(pr_hbm.at[1], pr)
        b_both[1] = pass_on(gbr, 1, b_far[1])
        scan_back(0)
        norm_offers = [
            spread(lambda t: dot_nt(hid[0, t], w_i[...]), keep_b, 1, sib_b, 0, []),
            None,
        ]
        down = sum_y("down", w_d, down)
        norm_far = [owed(norm_offers[0], keep_b, sib_b, far_b, 0), None]
        b_near[1].wait_recv()
        b_both[1].wait_recv()
        heads_back(1, 0)
        heads_back(1, 1)
        fetch.wait()
        attend_back(1)
        scan_back(1)
        remote.sent(back_far[1])
        norm_offers[1] = spread(
            lambda t: dot_nt(hid[1, t], w_i[...]), keep_b, 1, sib_b, 1, norm_offers[0]
        )
        up = sum_y("up", w_u, up)
        norm_far[1] = owed(norm_offers[1], keep_b, sib_b, far_b, 1)
        out_far[1] = owed(out_offers[1], keep_a, sib_a, far_a, 1)
        tiles(xn, hid, w_i, 1 - y)
        inp = swap_y("inp", w_i)
        down = sum_z("down", w_d, down)
        tiles(xn, hid, w_i, y)
        gather_tile(ho, gbr, 0)
        for j in range(width // chans):
            misc[j * chans : (j + 1) * chans, :] = acc[:, j * chans : (j + 1) * chans].astype(BF16)
        ends = [mix(0, summed(out_offers[0], out_far[0], keep_a, sib_a, far_a, 0))]
        ends.append(
            norm_first_back(0, summed(norm_offers[0], norm_far[0], keep_b, sib_b, far_b, 0))
        )
        down = spread_y("down", down)
        ends.append(mix(1, summed(out_offers[1], out_far[1], keep_a, sib_a, far_a, 1)))
        ends.append(
            norm_first_back(1, summed(norm_offers[1], norm_far[1], keep_b, sib_b, far_b, 1))
        )
        gains = [
            remote.start(gain_acc, gain_got.at[k], device)
            for k, device in enumerate((to_near, to_far, to_both))
        ]
        up = sum_z("up", w_u, up)
        base = width
        for h in range(heads):
            misc[base + h * CTX : base + (h + 1) * CTX, :] = (gcw[0, h] + gcw[1, h]).astype(BF16)
        base += heads * CTX
        for k in range(3):
            misc[base + k * NS : base + (k + 1) * NS, :] = (gss[0, k] + gss[1, k]).astype(BF16)
        base += 3 * NS
        for copy in gains:
            copy.wait_recv()
        value = gain_acc[...] + gain_got[0] + gain_got[1] + gain_got[2]
        tail_rows = misc_rows - base
        line = jnp.concatenate(
            [value[r : r + 1, j * chans : (j + 1) * chans] for r in range(2) for j in range(4)],
            axis=0,
        )
        misc[base:, :] = jnp.concatenate(
            [line, jnp.zeros((tail_rows - 8, chans), F32)], axis=0
        ).astype(BF16)
        mis = swap_y("misc", misc)
        inp = sum_y("inp", w_i, inp)
        up = spread_y("up", up)
        mis = sum_y("misc", misc, mis)
        inp = sum_z("inp", w_i, inp)
        mis = sum_z("misc", misc, mis)
        inp = spread_y("inp", inp)
        mis = spread_y("misc", mis)
        for state in (down, up, inp, mis):
            finish(state)
        for end in ends:
            end.wait()
        remote.drain()
        assert remote.used <= n_remote and local.used <= n_local, (remote.used, local.used)

    pieces = (count, 4, rows)
    vm = pltpu.VMEM
    any_out = [
        shape((count, rows, width), BF16),
        shape((count, rows, width), F32),
        shape((count, heads, 2, BLK, BLK + CTX), BF16),
    ]
    any_out += [shape(sizes[n], BF16) for n in names]
    any_out += [shape((sizes[n][0] // 2, sizes[n][1]), BF16) for n in names]
    any_out += [
        shape((nz - 1, sizes[n][0] // 2 // nz, sizes[n][1]), BF16) for n in names
    ]
    results = pl.pallas_call(
        kernel,
        in_specs=[SMEM, VMEM, ANY, VMEM, VMEM, ANY, VMEM, VMEM, VMEM, VMEM, ANY, ANY, ANY],
        out_specs=[ANY] * len(any_out),
        out_shape=any_out,
        scratch_shapes=[
            vm(w_in.shape, BF16),
            vm(w_out.shape, BF16),
            vm(w_up.shape, BF16),
            vm(w_down.shape, BF16),
            vm(pieces + (width,), BF16),
            vm(pieces + (width,), BF16),
            vm(pieces + (width,), BF16),
            vm(pieces + (width,), BF16),
            vm(pieces + (hidden,), BF16),
            vm(pieces + (hidden,), BF16),
            vm((count, total, 3 * chans), BF16),
            vm((count, BLK, chans), F32),
            vm((heads, 2, BLK, BLK + CTX), BF16),
            vm(pieces + (chans,), BF16),
            vm((count, CTX, chans), BF16),
            vm((count, heads, CTX, 2 * HD), BF16),
            vm((total, chans), BF16),
            vm((CTX, chans), F32),
            vm((2, 2, rows, width), BF16),
            vm((count, 2, rows, width), BF16),
            vm((count, 2, rows, width), BF16),
            vm((count, 2, rows, width), BF16),
            vm((count, 2, rows, width), BF16),
            vm((count, rows, width), BF16),
            vm((count, rows, width), BF16),
            vm((count, rows, width), F32),
            vm((rows, width), F32),
            vm((misc_rows // 2, chans), BF16),
            vm((misc_rows, chans), BF16),
            vm((8, width), F32),
            vm((3, 8, width), F32),
            vm((count, heads, CTX, 2 * HD), F32),
            vm((count, 3, NS, chans), F32),
            pltpu.SemaphoreType.DMA((n_remote,)),
            pltpu.SemaphoreType.DMA((n_remote,)),
            pltpu.SemaphoreType.DMA((n_local,)),
        ],
        compiler_params=pltpu.CompilerParams(
            collective_id=0, has_side_effects=True, vmem_limit_bytes=63 << 20
        ),
        cost_estimate=cost(45e9, 60e6),
    )(lengths, tokens, cotangent, gain_one, gain_two, w_in, *ssm, ctx_w, w_out, w_up, w_down)
    return results[0], results[1], dict(zip(names, results[3:7]))


def body(
    tokens,
    lengths,
    cotangent,
    attn_gain,
    in_weights,
    ssm_rate,
    ssm_input,
    ssm_output,
    ctx_weights,
    out_weights,
    mlp_gain,
    up_weights,
    down_weights,
):
    width = tokens.shape[2]
    chans = out_weights.shape[0]
    heads = ctx_weights.shape[0]
    mixed, grad_tokens, grads = layer(
        lax.axis_size("dp") // 2,
        tokens,
        lengths[0],
        cotangent,
        attn_gain.reshape(1, width),
        mlp_gain.reshape(1, width),
        in_weights.reshape(width, 4 * chans),
        (ssm_rate, ssm_input, ssm_output),
        ctx_weights,
        out_weights,
        up_weights,
        down_weights,
    )
    misc = grads["misc"].astype(F32)
    parts = width // chans
    grad_out = jnp.concatenate([misc[j * chans : (j + 1) * chans] for j in range(parts)], axis=1)
    at = width
    grad_ctx = misc[at : at + heads * CTX].reshape(ctx_weights.shape)
    at += heads * CTX
    grad_ssm = misc[at : at + 3 * NS].reshape(3, NS, chans)
    at += 3 * NS
    gains = misc[at : at + 2 * parts].reshape(2, width)
    return (
        mixed,
        grad_tokens,
        gains[0],
        grads["inp"].astype(F32).reshape(in_weights.shape),
        grad_ssm[0],
        grad_ssm[1],
        grad_ssm[2],
        grad_ctx,
        grad_out,
        gains[1],
        grads["up"].astype(F32),
        grads["down"].astype(F32),
    )


def solution(mesh):
    rows = P(None, ("dp", "mp"), None)
    return jax.shard_map(
        body,
        mesh=mesh,
        in_specs=(
            rows,
            P("dp", None, None),
            rows,
            P(),
            P(None, None, "mp"),
            P(None, "mp"),
            P(None, "mp"),
            P(None, "mp"),
            P("mp", None, None),
            P("mp", None),
            P(),
            P(None, "mp"),
            P("mp", None),
        ),
        out_specs=(
            rows,
            rows,
            P(),
            P(None, None, "mp"),
            P(None, "mp"),
            P(None, "mp"),
            P(None, "mp"),
            P("mp", None, None),
            P("mp", None),
            P(),
            P(None, "mp"),
            P("mp", None),
        ),
        check_vma=False,
    )
```

time: 1450 us -> 364 us (0.25)
  the two profiles are of different devices: /device:TPU:0 before, /device:TPU:18 now
where the time goes in v2:
time: 364 us; the launch traced here: 358 us
  Pallas kernels  334 us (92%)
  local copies, waits for them, and re-layouts  16.4 us (5%)
  other arithmetic  6.15 us (2%)
    pallas_call x1, Pallas kernels, layer(): pl.pallas_call(kernel, in_specs=[SMEM, VMEM, ANY, VMEM, VMEM, ANY, VMEM,...  334 us
    unnamed x16, local copies, waits for them, and re-layouts  7.91 us

profile of v2, /device:TPU:18, one launch (start us, length us, event | category | flops | bytes accessed | tf_op | source)
XLA Modules:
  0.0 357.7 jit_solution(7630238198666684774)
XLA Ops:
  0.6 3.4 copy.25
  4.1 334.0 %shard_map.220 = (bf16[2,256,1024]{2,1,0:T(8,128)(2,1)}, f32[2,256,1024]{2,1,0:T(8,128)}, bf16[2,2,2,512,640]{4,3,2,1,0:T(8,128)(2,1)}, bf16[1024,1024]{1,0:T(8,...) custom-call(s32[2,2]{1,0:T(2,128)} %bitcast.19, ...), custom_call_target="tpu_custom_call" | custom-call | flops 44999999488 | bytes 60000000 | tf_op jit(solution)/shard_map/pallas_call | solution.py:820
  338.0 1.4 fusion.1
  339.4 0.0 copy-start
  339.4 2.0 fusion
  341.4 1.1 pad_maximum_fusion
  342.5 0.0 copy-done
  342.5 0.1 convert_element_type.10
  342.6 0.6 copy.27
  343.2 0.6 copy.26
  343.8 0.0 copy-start.2
  343.8 5.1 %reshape.61 = f32[1024,4,256]{2,1,0:T(4,128)} reshape(bf16[1024,1024]{1,0:T(8,128)(2,1)} %get-tuple-element.21) | data formatting | bytes 6291456 | tf_op jit(solution)/shard_map/reshape | solution.py:916
  349.0 0.0 copy-done.2
  349.0 0.0 copy-start.1
  349.0 2.5 convert_element_type.11
  351.4 0.0 copy-done.1
  351.4 0.0 copy-start.4
  351.4 2.5 convert_element_type.12
  353.9 0.0 copy-done.4
  353.9 0.0 copy-start.3
  353.9 1.0 copy.30
  354.9 1.0 copy-done.3
  355.9 1.3 copy.31
  (1 shorter events, 0.0 us)
Async XLA Ops:
  339.4 3.1 copy-start
  343.8 5.1 %copy-start.2 = (bf16[1024,1024]{1,0:T(8,128)(2,1)S(1)}, bf16[1024,1024]{1,0:T(8,128)(2,1)}, u32[]{:S(2)}) copy-start(bf16[1024,1024]{1,0:T(8,128)(2,1)} %get-tuple-element.22) | copy-start | bytes 6291460
  349.0 2.5 copy-start.1
  351.4 2.5 copy-start.4
  353.9 2.0 copy-start.3
